TPU v7x, 32 devices: a whole 2x2x4 slice. The times are simulated.
32 devices in a mesh: pipe: 2 (over x), dp: 8 (over z, y), tensor: 2 (over core).
Axes of the slice: x: 2, y: 2, z: 4, core: 2. Of those that a mesh axis runs over, the one named last changes fastest.
Arguments:
- tokens: bfloat16 [1024, 2048], P('dp'), may hold values from -6 to 6
- cotangent: bfloat16 [1024, 2048], P('dp'), may hold values from -6 to 6
- attn_gain: bfloat16 [2, 2048], P('pipe', 'dp'), may hold values from 0.5 to 1.5
- w_query: bfloat16 [2, 2048, 2048], P('pipe', 'dp', 'tensor'), may hold values from -0.125 to 0.125
- w_key: bfloat16 [2, 2048, 512], P('pipe', 'dp', 'tensor'), may hold values from -0.125 to 0.125
- w_value: bfloat16 [2, 2048, 512], P('pipe', 'dp', 'tensor'), may hold values from -0.125 to 0.125
- w_out: bfloat16 [2, 2048, 2048], P('pipe', 'tensor', 'dp'), may hold values from -0.375 to 0.375
- mlp_gain: bfloat16 [2, 2048], P('pipe', 'dp'), may hold values from 0.5 to 1.5
- w_gate: bfloat16 [2, 2048, 8192], P('pipe', 'dp', 'tensor'), may hold values from -0.125 to 0.125
- w_up: bfloat16 [2, 2048, 8192], P('pipe', 'dp', 'tensor'), may hold values from -0.125 to 0.125
- w_down: bfloat16 [2, 8192, 2048], P('pipe', 'tensor', 'dp'), may hold values from -0.0625 to 0.0625
Outputs:
- activations: bfloat16 [2, 1024, 2048], P('pipe', 'dp')
- input_grads: float32 [2, 1024, 2048], P('pipe', 'dp')
- grad_attn_gain: float32 [2, 2048], P('pipe', 'dp')
- grad_query: float32 [2, 2048, 2048], P('pipe', 'dp', 'tensor')
- grad_key: float32 [2, 2048, 512], P('pipe', 'dp', 'tensor')
- grad_value: float32 [2, 2048, 512], P('pipe', 'dp', 'tensor')
- grad_out: float32 [2, 2048, 2048], P('pipe', 'tensor', 'dp')
- grad_mlp_gain: float32 [2, 2048], P('pipe', 'dp')
- grad_gate: float32 [2, 2048, 8192], P('pipe', 'dp', 'tensor')
- grad_up: float32 [2, 2048, 8192], P('pipe', 'dp', 'tensor')
- grad_down: float32 [2, 8192, 2048], P('pipe', 'tensor', 'dp')
All inputs are finite; a program needn't handle non-finite values.
Results may differ from a plain program's by a relative error of at most 0.03.
Values may be sent and summed in bfloat16 or wider, within the bound.
No kernel may reach another device: no remote copies, remote signals or barrier semaphores. Data moves between devices by JAX's collectives and lax.ppermute only.
A program may use at most 512 MiB of HBM per device.

v0:
```python
import jax
import jax.numpy as jnp
from jax import lax
from jax.sharding import PartitionSpec as P

HEAD = 64
MB = 2


eps = 1e-05
theta = 500000.0


def shifted(block, axis, distance):
    devices = range(lax.axis_size(axis))
    route = [(i - distance, i) for i in devices if i - distance in devices]
    return lax.ppermute(block, axis, route)


def rope_angles(first_row, row_count, head_size):
    positions = (first_row + jnp.arange(row_count, dtype=jnp.int32)).astype(jnp.float32)
    inv_freq = theta ** (-jnp.arange(0, head_size // 2, dtype=jnp.float32) * 2.0 / head_size)
    angles = positions[:, None] * inv_freq[None, :]
    return (jnp.cos(angles)[:, None, :], jnp.sin(angles)[:, None, :])


def rotate(vector, cosine, sine_table):
    half_size = vector.shape[-1] // 2
    front_half = vector[..., :half_size]
    back_half = vector[..., half_size:]
    return jnp.concatenate(
        [
            front_half * cosine - back_half * sine_table,
            front_half * sine_table + back_half * cosine,
        ],
        axis=-1,
    )


def normed(vector, gain_vec):
    return vector * lax.rsqrt(jnp.mean(vector * vector, axis=-1, keepdims=True) + eps) * gain_vec


def gated_units(gate_pre, up_pre):
    return jax.nn.silu(gate_pre) * up_pre


def against(left_side, matrix):
    return lax.dot_general(
        left_side, matrix, (((1,), (1,)), ((), ())), preferred_element_type=jnp.float32
    )


def outer_product(left_side, right_side):
    return lax.dot_general(
        left_side, right_side, (((0,), (0,)), ((), ())), preferred_element_type=jnp.float32
    )


def store_rows(buffer, vector, row_start, is_valid):
    previous = lax.dynamic_slice_in_dim(buffer, row_start, vector.shape[0], 0)
    return lax.dynamic_update_slice_in_dim(
        buffer, jnp.where(is_valid, vector, previous), row_start, 0
    )


def unpack_weights(fetched_rows, fetched_cols):
    return (
        fetched_rows[0][0].astype(jnp.float32),
        fetched_rows[1][0].astype(jnp.float32),
        fetched_rows[2][0],
        fetched_rows[3][0],
        fetched_rows[4][0],
        fetched_rows[5][0],
        fetched_rows[6][0],
        fetched_cols[0][0],
        fetched_cols[1][0],
    )


def on_device(
    tokens, cotangent, attn_gain, w_query, w_key, w_value, w_out, mlp_gain, w_gate, w_up, w_down
):
    f32 = jnp.float32
    bf16 = jnp.bfloat16
    section_index = lax.axis_index("pipe")
    seq_len, model_width = tokens.shape
    blocks = MB
    tok_rows = seq_len // blocks
    head_size = HEAD
    q_width = w_query.shape[2]
    kv_width = w_key.shape[2]
    ff_local = w_gate.shape[2]
    kv_heads = kv_width // head_size
    group_size = q_width // kv_width
    score_scale = head_size ** (-0.5)
    fetched_rows = (
        lax.all_gather(attn_gain, "dp", axis=1, tiled=True),
        lax.all_gather(mlp_gain, "dp", axis=1, tiled=True),
        lax.all_gather(w_query, "dp", axis=1, tiled=True),
        lax.all_gather(w_key, "dp", axis=1, tiled=True),
        lax.all_gather(w_value, "dp", axis=1, tiled=True),
        lax.all_gather(w_gate, "dp", axis=1, tiled=True),
        lax.all_gather(w_up, "dp", axis=1, tiled=True),
    )
    fetched_cols = (
        lax.all_gather(w_out, "dp", axis=2, tiled=True),
        lax.all_gather(w_down, "dp", axis=2, tiled=True),
    )
    gain_one, gain_two, wq_full, wk_full, wv_full, wg_full, wu_full, wo_full, wd_full = (
        unpack_weights(fetched_rows, fetched_cols)
    )

    def masked_scores(q_rot, key_store, first_row):
        grouped = q_rot.reshape(tok_rows, kv_heads, group_size, head_size)
        key_rows = key_store.reshape(seq_len, kv_heads, head_size)
        scores = (
            jnp.einsum("qgrd,kgd->grqk", grouped, key_rows, preferred_element_type=f32)
            * score_scale
        )
        allowed = jnp.arange(seq_len)[None, :] <= (first_row + jnp.arange(tok_rows))[:, None]
        return jnp.where(allowed, scores, -1e30)

    in_store = jnp.zeros((seq_len, model_width), bf16)
    middle_store = jnp.zeros((seq_len, model_width), f32)
    xn_one_store = jnp.zeros((seq_len, model_width), bf16)
    xn_two_store = jnp.zeros((seq_len, model_width), bf16)
    qrot_store = jnp.zeros((seq_len, q_width), bf16)
    key_store = jnp.zeros((seq_len, kv_width), bf16)
    value_store = jnp.zeros((seq_len, kv_width), bf16)
    mixed_store = jnp.zeros((seq_len, q_width), bf16)
    gate_store = jnp.zeros((seq_len, ff_local), f32)
    up_store = jnp.zeros((seq_len, ff_local), f32)
    hidden_store = jnp.zeros((seq_len, ff_local), bf16)
    total_store = jnp.zeros((blocks, kv_heads, group_size, tok_rows, 1), f32)
    output_store = jnp.zeros((seq_len, model_width), bf16)
    incoming = jnp.zeros((tok_rows, model_width), bf16)
    for tick_index in range(blocks + 1):
        slot_index = tick_index - section_index
        is_valid = jnp.logical_and(slot_index >= 0, slot_index < blocks)
        slot_index = jnp.clip(slot_index, 0, blocks - 1)
        first_row = slot_index * tok_rows
        own_rows = lax.dynamic_slice_in_dim(tokens, first_row, tok_rows, 0)
        layer_in = jnp.where(section_index == 0, own_rows, incoming)
        cosine, sine_table = rope_angles(first_row, tok_rows, head_size)
        residual = layer_in.astype(f32)
        xn_one = normed(residual, gain_one).astype(bf16)
        q_all = jnp.dot(xn_one, wq_full, preferred_element_type=f32)
        k_all = jnp.dot(xn_one, wk_full, preferred_element_type=f32)
        v_all = jnp.dot(xn_one, wv_full, preferred_element_type=f32).astype(bf16)
        q_rot = (
            rotate(q_all.reshape(tok_rows, -1, head_size), cosine, sine_table)
            .astype(bf16)
            .reshape(tok_rows, q_width)
        )
        k_rot = (
            rotate(k_all.reshape(tok_rows, -1, head_size), cosine, sine_table)
            .astype(bf16)
            .reshape(tok_rows, kv_width)
        )
        key_store = store_rows(key_store, k_rot, first_row, is_valid)
        value_store = store_rows(value_store, v_all, first_row, is_valid)
        scores = masked_scores(q_rot, key_store, first_row)
        row_max = jnp.max(scores, axis=-1, keepdims=True)
        expo = jnp.exp(scores - row_max)
        row_total = jnp.sum(expo, axis=-1, keepdims=True)
        log_total = row_max + jnp.log(row_total)
        attn_probs = (expo / row_total).astype(bf16)
        value_rows = value_store.reshape(seq_len, kv_heads, head_size)
        attn_mixed = jnp.einsum(
            "grqk,kgd->qgrd", attn_probs, value_rows, preferred_element_type=f32
        )
        attn_mixed = attn_mixed.astype(bf16).reshape(tok_rows, q_width)
        head_part = jnp.dot(attn_mixed, wo_full, preferred_element_type=f32)
        middle = residual + lax.psum(head_part, "tensor")
        xn_two = normed(middle, gain_two).astype(bf16)
        gate_pre = jnp.dot(xn_two, wg_full, preferred_element_type=f32)
        up_pre = jnp.dot(xn_two, wu_full, preferred_element_type=f32)
        hidden = gated_units(gate_pre, up_pre).astype(bf16)
        unit_part = jnp.dot(hidden, wd_full, preferred_element_type=f32)
        layer_out = (middle + lax.psum(unit_part, "tensor")).astype(bf16)
        in_store = store_rows(in_store, layer_in, first_row, is_valid)
        middle_store = store_rows(middle_store, middle, first_row, is_valid)
        xn_one_store = store_rows(xn_one_store, xn_one, first_row, is_valid)
        xn_two_store = store_rows(xn_two_store, xn_two, first_row, is_valid)
        qrot_store = store_rows(qrot_store, q_rot, first_row, is_valid)
        mixed_store = store_rows(mixed_store, attn_mixed, first_row, is_valid)
        gate_store = store_rows(gate_store, gate_pre, first_row, is_valid)
        up_store = store_rows(up_store, up_pre, first_row, is_valid)
        hidden_store = store_rows(hidden_store, hidden, first_row, is_valid)
        total_store = store_rows(total_store, log_total[None], slot_index, is_valid)
        output_store = store_rows(output_store, layer_out, first_row, is_valid)
        if tick_index < blocks:
            incoming = shifted(layer_out, "pipe", 1)
    fetched_rows = (
        lax.all_gather(attn_gain, "dp", axis=1, tiled=True),
        lax.all_gather(mlp_gain, "dp", axis=1, tiled=True),
        lax.all_gather(w_query, "dp", axis=1, tiled=True),
        lax.all_gather(w_key, "dp", axis=1, tiled=True),
        lax.all_gather(w_value, "dp", axis=1, tiled=True),
        lax.all_gather(w_gate, "dp", axis=1, tiled=True),
        lax.all_gather(w_up, "dp", axis=1, tiled=True),
    )
    fetched_cols = (
        lax.all_gather(w_out, "dp", axis=2, tiled=True),
        lax.all_gather(w_down, "dp", axis=2, tiled=True),
    )
    gain_one, gain_two, wq_full, wk_full, wv_full, wg_full, wu_full, wo_full, wd_full = (
        unpack_weights(fetched_rows, fetched_cols)
    )
    grad_store = jnp.zeros((seq_len, model_width), f32)
    dqkv_store = jnp.zeros((seq_len, q_width + 2 * kv_width), bf16)
    dattn_store = jnp.zeros((seq_len, model_width), bf16)
    dunits_store = jnp.zeros((seq_len, 2 * ff_local), bf16)
    dmlp_store = jnp.zeros((seq_len, model_width), bf16)
    key_grads = jnp.zeros((seq_len, 2 * kv_width), f32)
    gain_acc_one = jnp.zeros((model_width,), f32)
    gain_acc_two = jnp.zeros((model_width,), f32)
    key_rows = key_store.reshape(seq_len, kv_heads, head_size)
    value_rows = value_store.reshape(seq_len, kv_heads, head_size)
    grad_in = jnp.zeros((tok_rows, model_width), bf16)
    for tick_index in range(blocks + 1):
        slot_index = blocks - section_index - tick_index
        is_valid = jnp.logical_and(slot_index >= 0, slot_index < blocks)
        slot_index = jnp.clip(slot_index, 0, blocks - 1)
        first_row = slot_index * tok_rows
        cosine, sine_table = rope_angles(first_row, tok_rows, head_size)
        from_cot = lax.dynamic_slice_in_dim(cotangent, first_row, tok_rows, 0)
        upstream = jnp.where(section_index == 1, from_cot, grad_in).astype(f32)
        middle = lax.dynamic_slice_in_dim(middle_store, first_row, tok_rows, 0)
        gate_pre = lax.dynamic_slice_in_dim(gate_store, first_row, tok_rows, 0)
        up_pre = lax.dynamic_slice_in_dim(up_store, first_row, tok_rows, 0)
        d_mlp = upstream.astype(bf16)
        d_hidden = against(d_mlp, wd_full)
        unit_value, unit_pull = jax.vjp(gated_units, gate_pre, up_pre)
        d_gate, d_up = unit_pull(d_hidden)
        d_gate = d_gate.astype(bf16)
        d_up = d_up.astype(bf16)
        d_xn_two = lax.psum(against(d_gate, wg_full) + against(d_up, wu_full), "tensor")
        norm_value, norm_pull = jax.vjp(normed, middle, gain_two)
        d_mid_norm, d_gain_two = norm_pull(d_xn_two)
        d_middle = upstream + d_mid_norm
        d_attn = d_middle.astype(bf16)
        d_mixed = against(d_attn, wo_full).astype(bf16)
        q_rot = lax.dynamic_slice_in_dim(qrot_store, first_row, tok_rows, 0)
        scores = masked_scores(q_rot, key_store, first_row)
        log_total = lax.dynamic_index_in_dim(total_store, slot_index, 0, keepdims=False)
        probs_full = jnp.exp(scores - log_total)
        attn_probs = probs_full.astype(bf16)
        d_grouped = d_mixed.reshape(tok_rows, kv_heads, group_size, head_size)
        q_grouped = q_rot.reshape(tok_rows, kv_heads, group_size, head_size)
        d_probs = jnp.einsum("qgrd,kgd->grqk", d_grouped, value_rows, preferred_element_type=f32)
        row_delta = jnp.sum(probs_full * d_probs, axis=-1, keepdims=True)
        d_scores = (probs_full * (d_probs - row_delta)).astype(bf16)
        dq_rot = (
            jnp.einsum("grqk,kgd->qgrd", d_scores, key_rows, preferred_element_type=f32)
            * score_scale
        )
        dk_rot = (
            jnp.einsum("grqk,qgrd->kgd", d_scores, q_grouped, preferred_element_type=f32)
            * score_scale
        )
        dv_part = jnp.einsum("grqk,qgrd->kgd", attn_probs, d_grouped, preferred_element_type=f32)
        contribution = jnp.concatenate(
            [dk_rot.reshape(seq_len, kv_width), dv_part.reshape(seq_len, kv_width)], axis=1
        )
        key_grads = key_grads + jnp.where(is_valid, contribution, 0.0)
        own_key_grads = lax.dynamic_slice_in_dim(key_grads, first_row, tok_rows, 0)
        d_query = (
            rotate(dq_rot.reshape(tok_rows, -1, head_size), cosine, -sine_table)
            .astype(bf16)
            .reshape(tok_rows, q_width)
        )
        d_key = rotate(
            own_key_grads[:, :kv_width].reshape(tok_rows, -1, head_size), cosine, -sine_table
        )
        d_key = d_key.astype(bf16).reshape(tok_rows, kv_width)
        d_value = own_key_grads[:, kv_width:].astype(bf16)
        d_xn_one = against(d_query, wq_full) + against(d_key, wk_full) + against(d_value, wv_full)
        d_xn_one = lax.psum(d_xn_one.astype(jnp.bfloat16), "tensor").astype(jnp.float32)
        layer_in = lax.dynamic_slice_in_dim(in_store, first_row, tok_rows, 0).astype(f32)
        norm_value, norm_pull = jax.vjp(normed, layer_in, gain_one)
        d_in_norm, d_gain_one = norm_pull(d_xn_one)
        d_input = d_middle + d_in_norm
        d_input_low = d_input.astype(bf16)
        grad_store = store_rows(
            grad_store,
            jnp.where(section_index == 1, d_input_low.astype(f32), d_input),
            first_row,
            is_valid,
        )
        dqkv_store = store_rows(
            dqkv_store, jnp.concatenate([d_query, d_key, d_value], axis=1), first_row, is_valid
        )
        dattn_store = store_rows(dattn_store, d_attn, first_row, is_valid)
        dunits_store = store_rows(
            dunits_store, jnp.concatenate([d_gate, d_up], axis=1), first_row, is_valid
        )
        dmlp_store = store_rows(dmlp_store, d_mlp, first_row, is_valid)
        gain_acc_one = gain_acc_one + jnp.where(is_valid, d_gain_one, 0.0)
        gain_acc_two = gain_acc_two + jnp.where(is_valid, d_gain_two, 0.0)
        if tick_index < blocks:
            grad_in = shifted(d_input_low, "pipe", -1)
    term_parts = [
        outer_product(xn_one_store, dqkv_store),
        outer_product(xn_two_store, dunits_store),
        outer_product(dattn_store, mixed_store),
        outer_product(dmlp_store, hidden_store),
        gain_acc_one[:, None],
        gain_acc_two[:, None],
    ]
    summed = lax.psum_scatter(
        jnp.concatenate(term_parts, axis=1).astype(jnp.bfloat16),
        "dp",
        scatter_dimension=0,
        tiled=True,
    ).astype(jnp.float32)
    offset_units = q_width + 2 * kv_width
    offset_out = offset_units + 2 * ff_local
    offset_down = offset_out + q_width
    offset_gain = offset_down + ff_local
    qkv_part = summed[:, :offset_units]
    units_part = summed[:, offset_units:offset_out]
    out_part = summed[:, offset_out:offset_down]
    down_part = summed[:, offset_down:offset_gain]
    gain_first = summed[:, offset_gain]
    gain_second = summed[:, offset_gain + 1]
    grad_query = qkv_part[:, :q_width][None]
    grad_key = qkv_part[:, q_width : q_width + kv_width][None]
    grad_value = qkv_part[:, q_width + kv_width :][None]
    grad_gate = units_part[:, :ff_local][None]
    grad_up = units_part[:, ff_local:][None]
    grad_out = out_part.T[None]
    grad_down = down_part.T[None]
    grad_attn_gain = gain_first[None]
    grad_mlp_gain = gain_second[None]
    return (
        output_store[None],
        grad_store[None],
        grad_attn_gain,
        grad_query,
        grad_key,
        grad_value,
        grad_out,
        grad_mlp_gain,
        grad_gate,
        grad_up,
        grad_down,
    )


def solution(mesh):
    in_specs = (
        P("dp", None),
        P("dp", None),
        P("pipe", "dp"),
        P("pipe", "dp", "tensor"),
        P("pipe", "dp", "tensor"),
        P("pipe", "dp", "tensor"),
        P("pipe", "tensor", "dp"),
        P("pipe", "dp"),
        P("pipe", "dp", "tensor"),
        P("pipe", "dp", "tensor"),
        P("pipe", "tensor", "dp"),
    )
    out_specs = (
        P("pipe", "dp", None),
        P("pipe", "dp", None),
        P("pipe", "dp"),
        P("pipe", "dp", "tensor"),
        P("pipe", "dp", "tensor"),
        P("pipe", "dp", "tensor"),
        P("pipe", "tensor", "dp"),
        P("pipe", "dp"),
        P("pipe", "dp", "tensor"),
        P("pipe", "dp", "tensor"),
        P("pipe", "tensor", "dp"),
    )
    return jax.shard_map(
        on_device, mesh=mesh, in_specs=in_specs, out_specs=out_specs, check_vma=False
    )
```

profile of v0, /device:TPU:0, one launch (start us, length us, event | category | flops | bytes accessed | tf_op | source)
XLA Modules:
  0.0 2575.9 jit_solution(17640607788023667417)
XLA Ops:
  10.1 22.5 all_gather.36
  35.2 17.9 all-gather.8.cloned.1.call-done
  54.9 39.3 %all-gather.10.cloned.1.call-done = bf16[1,2048,256]{2,1,0:T(8,128)(2,1)} async-done(((bf16[1,256,256]{2,1,0:T(8,128)(2,1)}), bf16[1,2048,256]{2,1,0:T(8,128)(2,1)}) %all-gather.10.cloned.1.call-update) | async-done | bytes 1048592 | tf_op jit(solution)/shard_map/all_gather | solution.py:101
  96.6 72.0 %all-gather.12.cloned.1.call-done = bf16[1,2048,1024]{2,1,0:T(8,128)(2,1)} async-done(((bf16[1,256,1024]{2,1,0:T(8,128)(2,1)}), bf16[1,2048,1024]{2,1,0:T(8,128)(2,1)}) %all-gather.12.cloned.1.call-update) | async-done | bytes 4194320 | tf_op jit(solution)/shard_map/all_gather | solution.py:100
  180.6 63.1 %all-gather.14.cloned.1.call-done = bf16[1,1024,2048]{2,1,0:T(8,128)(2,1)} async-done(((bf16[1,1024,256]{2,1,0:T(8,128)(2,1)}), bf16[1,1024,2048]{2,1,0:T(8,128)(2,1)}) %all-gather.14.cloned.1.call-update) | async-done | bytes 4194320 | tf_op jit(solution)/shard_map/all_gather | solution.py:107
  249.8 17.9 all_gather.41
  272.9 222.9 %all-gather.16.cloned.1.call-done = bf16[1,2048,4096]{2,1,0:T(8,128)(2,1)} async-done(((bf16[1,256,4096]{2,1,0:T(8,128)(2,1)}), bf16[1,2048,4096]{2,1,0:T(8,128)(2,1)}) %all-gather.16.cloned.1.call-update) | async-done | bytes 16777232 | tf_op jit(solution)/shard_map/all_gather | solution.py:103
  507.4 216.5 %all-gather.18.cloned.1.call-done = bf16[1,2048,4096]{2,1,0:T(8,128)(2,1)} async-done(((bf16[1,256,4096]{2,1,0:T(8,128)(2,1)}), bf16[1,2048,4096]{2,1,0:T(8,128)(2,1)}) %all-gather.18.cloned.1.call-update) | async-done | bytes 16777232 | tf_op jit(solution)/shard_map/all_gather | solution.py:104
  735.3 216.9 %all-gather.20.cloned.1.call-done = bf16[1,4096,2048]{2,1,0:T(8,128)(2,1)} async-done(((bf16[1,4096,256]{2,1,0:T(8,128)(2,1)}), bf16[1,4096,2048]{2,1,0:T(8,128)(2,1)}) %all-gather.20.cloned.1.call-update) | async-done | bytes 16777232 | tf_op jit(solution)/shard_map/all_gather | solution.py:108
  964.8 14.1 all-reduce.15.cloned.1.call-done
  1022.4 14.8 all-reduce.17.cloned.1.call-done
  1071.2 13.2 all-reduce.19.cloned.1.call-done
  1166.0 12.5 fusion.128
  1190.1 11.8 fusion.72
  1203.6 18.4 all-reduce.23.cloned.1.call-done
  1273.3 12.7 fusion.131
  1297.2 11.8 fusion.75
  1350.4 17.2 all-reduce.29.cloned.1.call-done
  1385.0 12.6 fusion.134
  1411.6 11.8 fusion.78
  1423.4 16.3 convolution_convert_fusion
  1439.7 11.8 convolution_convert_fusion.1
  1499.8 84.4 %concatenate.127 = bf16[2048,14850]{1,0:T(8,128)(2,1)} concatenate(bf16[2048,1536]{1,0:T(8,128)(2,1)} %copy.97, bf16[2048,8192]{1,0:T(8,128)(2,1)} %convolution_convert_fusion, bf16[2048,1024]{1,0:T(8,128)(2,1)} %convolution_convert_fusion.3, bf16[2048,4096]{1,0:T(8,128)(2,1)} %convolution_convert_fusion.1, bf16[2048,1]{1,0:T(8,128)(2,1)S(1)} %add.623, bf16[2048,1]{1,0:T(8,128)(2,1)S(1)} %add.624), dimensions={1} | concatenate | bytes 121651200 | tf_op jit(solution)/shard_map/concatenate | solution.py:313
  1590.7 946.0 %reduce-scatter.2.cloned.1.call-done = bf16[256,14850]{1,0:T(8,128)(2,1)} async-done(((bf16[2048,14850]{1,0:T(8,128)(2,1)}), bf16[256,14850]{1,0:T(8,128)(2,1)}) %reduce-scatter.2.cloned.1.call-update) | async-done | bytes 7603216 | tf_op jit(solution)/shard_map/reduce_scatter | solution.py:312
  (523 shorter events, 461.4 us)
Async XLA Ops:
  7.2 46.0 %all-gather.8.cloned.1.call-start = ((), (), s32[]{:S(2)}) async-start(), calls=%async_computation.1 | async-start | bytes 1179648 | tf_op jit(solution)/shard_map/all_gather | solution.py:102
  7.9 86.3 %all-gather.10.cloned.1.call-start = ((), (), s32[]{:S(2)}) async-start(), calls=%async_computation.2 | async-start | bytes 1179648 | tf_op jit(solution)/shard_map/all_gather | solution.py:101
  8.7 159.9 %all-gather.12.cloned.1.call-start = ((), (), s32[]{:S(2)}) async-start(), calls=%async_computation.3 | async-start | bytes 4718592 | tf_op jit(solution)/shard_map/all_gather | solution.py:100
  9.4 234.3 %all-gather.14.cloned.1.call-start = ((), (), s32[]{:S(2)}) async-start(), calls=%async_computation.4 | async-start | bytes 4718592 | tf_op jit(solution)/shard_map/all_gather | solution.py:107
  10.0 260.2 %all-reduce.13.cloned.1.call-start = ((), (), s32[]{:S(2)}) async-start(), calls=%async_computation.5 | async-start | bytes 1048576 | tf_op jit(solution)/shard_map/psum | solution.py:175
  247.6 248.1 %all-gather.16.cloned.1.call-start = ((), (), s32[]{:S(2)}) async-start(), calls=%async_computation.6 | async-start | bytes 18874368 | tf_op jit(solution)/shard_map/all_gather | solution.py:103
  248.2 475.7 %all-gather.18.cloned.1.call-start = ((), (), s32[]{:S(2)}) async-start(), calls=%async_computation.7 | async-start | bytes 18874368 | tf_op jit(solution)/shard_map/all_gather | solution.py:104
  249.0 703.1 %all-gather.20.cloned.1.call-start = ((), (), s32[]{:S(2)}) async-start(), calls=%async_computation.8 | async-start | bytes 18874368 | tf_op jit(solution)/shard_map/all_gather | solution.py:108
  249.7 729.1 %all-reduce.15.cloned.1.call-start = ((), (), s32[]{:S(2)}) async-start(), calls=%async_computation.9 | async-start | bytes 1048576 | tf_op jit(solution)/shard_map/psum | solution.py:181
  272.8 234.5 %copy-start.13 = (bf16[128,2048]{1,0:T(8,128)(2,1)}, bf16[128,2048]{1,0:T(8,128)(2,1)S(1)}, u32[]{:S(2)}) copy-start(bf16[128,2048]{1,0:T(8,128)(2,1)S(1)} %get-tuple-element.73) | copy-start | bytes 1572868
  961.8 75.5 %all-reduce.17.cloned.1.call-start = ((), (), s32[]{:S(2)}) async-start(), calls=%async_computation.10 | async-start | bytes 1048576 | tf_op jit(solution)/shard_map/psum | solution.py:175
  980.8 10.0 collective-permute-start
  1015.5 68.9 %all-reduce.19.cloned.1.call-start = ((), (), s32[]{:S(2)}) async-start(), calls=%async_computation.11 | async-start | bytes 1048576 | tf_op jit(solution)/shard_map/psum | solution.py:181
  1064.4 75.6 %all-reduce.21.cloned.1.call-start = ((), (), s32[]{:S(2)}) async-start(), calls=%async_computation.12 | async-start | bytes 1048576 | tf_op jit(solution)/shard_map/psum | solution.py:175
  1086.5 9.6 collective-permute-start.1
  1119.2 102.9 %all-reduce.23.cloned.1.call-start = ((), (), s32[]{:S(2)}) async-start(), calls=%async_computation.13 | async-start | bytes 1048576 | tf_op jit(solution)/shard_map/psum | solution.py:239
  1202.0 54.0 %all-reduce.25.cloned.1.call-start = ((), (), s32[]{:S(2)}) async-start(), calls=%async_computation.14 | async-start | bytes 524288 | tf_op jit(solution)/shard_map/psum | solution.py:280
  1236.3 92.0 %all-reduce.27.cloned.1.call-start = ((), (), s32[]{:S(2)}) async-start(), calls=%async_computation.15 | async-start | bytes 1048576 | tf_op jit(solution)/shard_map/psum | solution.py:239
  1261.2 10.3 collective-permute-start.2
  1309.1 58.5 %all-reduce.29.cloned.1.call-start = ((), (), s32[]{:S(2)}) async-start(), calls=%async_computation.16 | async-start | bytes 524288 | tf_op jit(solution)/shard_map/psum | solution.py:280
  1348.0 103.5 %all-reduce.33.cloned.1.call-start = ((), (), s32[]{:S(2)}) async-start(), calls=%async_computation.19 | async-start | bytes 2097152 | tf_op jit(solution)/shard_map/psum | solution.py:181
  1372.4 10.6 collective-permute-start.3
  1423.4 74.8 %all-reduce.31.cloned.1.call-start = ((), (), s32[]{:S(2)}) async-start(), calls=%async_computation.17 | async-start | bytes 524288 | tf_op jit(solution)/shard_map/psum | solution.py:280
  1478.4 1058.2 %reduce-scatter.2.cloned.1.call-start = ((), (), s32[]{:S(2)}) async-start(), calls=%async_computation.18 | async-start | bytes 69009408 | tf_op jit(solution)/shard_map/reduce_scatter | solution.py:312
  (111 other events, 1746.4 us)
Sparse Core Ops, SparseCore 0:
  10.1 42.9 all-gather.7
  55.3 38.8 all-gather.9
  96.3 72.1 all-gather.11
  170.4 73.2 all-gather.13
  247.8 16.8 all-reduce.12
  266.9 228.7 all-gather.15
  498.1 225.7 all-gather.17
  726.1 225.9 all-gather.19
  961.9 16.8 all-reduce.14
  1015.6 21.5 all-reduce.16
  1064.5 19.9 all-reduce.18
  1119.3 20.6 all-reduce.20
  1202.1 19.9 all-reduce.22
  1236.4 19.5 all-reduce.24
  1309.2 19.0 all-reduce.26
  1348.1 19.4 all-reduce.28
  1423.5 20.9 all-reduce.32
  1478.6 19.5 all-reduce.30
  1584.4 952.1 reduce-scatter.1
where the time goes:
time: 2590 us; the launch traced here: 2580 us
  waiting for transfers between devices  1920 us (74%)
  matrix products  295 us (11%)
  local copies, waits for them, and re-layouts  189 us (7%)
  other arithmetic  100 us (4%)
  blocking collectives  40.5 us (2%)
    reduce_scatter x1, waiting for transfers between devices, on_device(): lax.psum_scatter(jnp.concatenate(term_parts, axis=1).astype(jnp.bfloat16)...  946 us
    all_gather x1, waiting for transfers between devices, on_device(): lax.all_gather(w_gate, 'dp', axis=1, tiled=True)  223 us
    all_gather x1, waiting for transfers between devices, on_device(): lax.all_gather(w_down, 'dp', axis=2, tiled=True)  217 us
    all_gather x1, waiting for transfers between devices, on_device(): lax.all_gather(w_up, 'dp', axis=1, tiled=True)  217 us
    dot_general x21, matrix products, against(): lax.dot_general(left_side, matrix, (((1,), (1,)), ((), ())), preferred_el...  130 us
    concatenate x1, local copies, waits for them, and re-layouts, on_device(): jnp.concatenate(term_parts, axis=1).astype(jnp.bfloat16)  84.4 us
    all_gather x1, waiting for transfers between devices, on_device(): lax.all_gather(w_query, 'dp', axis=1, tiled=True)  72 us
    all_gather x1, waiting for transfers between devices, on_device(): lax.all_gather(w_out, 'dp', axis=2, tiled=True)  63.1 us
  transfers between devices with their start and end apart: 23, of which 21 were waited for; matrix products, arithmetic and copies ran while one was open for 6% of the time, Pallas kernels for 0%

commit v1 on v0

v1 whole, which is shorter than its diff:
```python
import jax
import jax.numpy as jnp
from jax import lax
from jax.experimental import pallas as pl
from jax.experimental.pallas import tpu as pltpu
from jax.sharding import PartitionSpec as P

HEAD = 64
LANES = 128
EPS = 1e-05
THETA = 500000.0
GROUPS = 2
VMEM_BYTES = 56 * 1024 * 1024
f32 = jnp.float32
bf16 = jnp.bfloat16


def rope_tables(positions):
    inv_freq = THETA ** (-jnp.arange(0, HEAD // 2, dtype=f32) * 2.0 / HEAD)
    angles = positions.astype(f32)[:, None] * inv_freq[None, :]
    cosine, sine = jnp.cos(angles), jnp.sin(angles)
    return jnp.concatenate([cosine] * 4, axis=1), jnp.concatenate([-sine, sine] * 2, axis=1)


def normed(vector, gain):
    return vector * lax.rsqrt(jnp.mean(vector * vector, axis=-1, keepdims=True) + EPS) * gain


def gated_units(gate, up):
    return jax.nn.silu(gate) * up


def dot(a, b):
    return jnp.dot(a, b, preferred_element_type=f32)


def dot_nt(a, b):
    return lax.dot_general(a, b, (((1,), (1,)), ((), ())), preferred_element_type=f32)


def dot_tn(a, b):
    return lax.dot_general(a, b, (((0,), (0,)), ((), ())), preferred_element_type=f32)


def to_core(block):
    return lax.ppermute(block, "tensor", [(0, 1), (1, 0)])


def to_plane(block):
    return lax.ppermute(block, "pipe", [(0, 1), (1, 0)])


def to_dp(block, flip):
    return lax.ppermute(block, "dp", [(i, i ^ flip) for i in range(lax.axis_size("dp"))])


def to_diagonal(block):
    n = lax.axis_size("dp")
    route = [(p * n + i, (1 - p) * n + (i ^ 1)) for p in range(2) for i in range(n)]
    return lax.ppermute(block, ("pipe", "dp"), route)


def column_groups():
    column = lax.axis_size("dp") // 2
    size = column // GROUPS
    return [range(g * size, (g + 1) * size) for g in range(GROUPS)]


def gather_tokens(block):
    out = []
    for group in column_groups():
        column = jnp.concatenate([block if k == 0 else to_dp(block, 2 * k) for k in group], axis=0)
        out.append(
            jnp.concatenate(
                [column, to_dp(column, 1), to_plane(column), to_diagonal(column)], axis=0
            )
        )
    return out


def sum_tokens(partials):
    total = None
    for group, (kept, beside, across, diagonal) in zip(column_groups(), partials):
        rows = kept.shape[0] // len(group)
        column = (
            kept
            + to_dp(beside, 1).astype(f32)
            + to_plane(across).astype(f32)
            + to_diagonal(diagonal).astype(f32)
        )
        for place, k in enumerate(group):
            part = column[place * rows : (place + 1) * rows]
            if k:
                part = to_dp(part.astype(bf16), 2 * k).astype(f32)
            total = part if total is None else total + part
    return total


def gather_four(block):
    pair = jnp.concatenate([block, to_plane(block)], axis=0)
    return jnp.concatenate([pair, to_core(pair)], axis=0)


def sum_four(kept, sent):
    pair = kept + to_core(sent).astype(f32)
    own = pair.shape[0] // 2
    return pair[:own] + to_plane(pair[own:].astype(bf16)).astype(f32)


def swapped_halves(tile):
    lane = lax.broadcasted_iota(jnp.int32, tile.shape, 1)
    up = pltpu.roll(tile, LANES - HEAD // 2, 1)
    down = pltpu.roll(tile, HEAD // 2, 1)
    return jnp.where(lane % HEAD < HEAD // 2, up, down)


def head_variants(tile):
    lane = lax.broadcasted_iota(jnp.int32, tile.shape, 1)
    low = jnp.where(lane < HEAD, tile, 0.0)
    high = jnp.where(lane < HEAD, 0.0, tile)
    turned = (pltpu.roll(low, HEAD, 1), pltpu.roll(high, HEAD, 1))
    return ((low.astype(bf16), turned[0].astype(bf16)), (turned[1].astype(bf16), high.astype(bf16)))


def softmax_rows(scores):
    expo = jnp.exp(scores - jnp.max(scores, axis=-1, keepdims=True))
    return expo / jnp.sum(expo, axis=-1, keepdims=True)


def listed(refs, count):
    if len(refs[0].shape) == 3:
        return [refs[0].at[j] for j in range(count)]
    return refs[:count]


def attend_forward_kernel(count, cols, q_width, offset_ref, x_ref, cos_ref, sin_ref, mask_ref, *refs):
    blocks = listed(refs, count)
    keep_ref, send_ref, q_ref, kv_ref, mixed_ref, xn_own_ref, gain_ref, xn_ref, full_ref = refs[-9:]
    rows = x_ref.shape[0]
    kv_width = LANES
    qkv_width = q_width + 2 * kv_width
    starts = [pl.multiple_of(offset_ref[j], cols) for j in range(count)]
    if count == 1:
        gain_ref[...] = refs[1][...].astype(f32)
    else:
        for start, block in zip(starts, blocks):
            gain_rows = block[cols:, :].astype(f32)
            for i in range(2):
                gain_ref[i : i + 1, pl.ds(start, cols)] = gain_rows[:1, i * cols : (i + 1) * cols]
    xn_ref[...] = normed(x_ref[...].astype(f32), gain_ref[0:1, :]).astype(bf16)
    xn_own_ref[...] = xn_ref[: xn_own_ref.shape[0], :]
    qkv = None
    for start, block in zip(starts, blocks):
        part = dot(xn_ref[:, pl.ds(start, cols)], block[:cols, :qkv_width])
        qkv = part if qkv is None else qkv + part
    cosine, sine, mask = cos_ref[...], sin_ref[...], mask_ref[...]

    def turned(tile):
        return tile * cosine + swapped_halves(tile) * sine

    keys = turned(qkv[:, q_width : q_width + kv_width]).astype(bf16)
    values = qkv[:, q_width + kv_width :].astype(bf16)
    kv_ref[:, :kv_width] = keys
    kv_ref[:, kv_width:] = values
    key_variants = head_variants(keys.astype(f32))
    value_variants = head_variants(values.astype(f32))
    tiles = q_width // LANES
    for i in range(tiles):
        kv_head = i * 2 // tiles
        tile = slice(i * LANES, (i + 1) * LANES)
        q_tile = turned(qkv[:, tile]).astype(bf16)
        q_ref[:, tile] = q_tile
        mixed = None
        for side in range(2):
            scores = dot_nt(q_tile, key_variants[kv_head][side]) * HEAD ** (-0.5) + mask
            part = dot(softmax_rows(scores).astype(bf16), value_variants[kv_head][side])
            mixed = part if mixed is None else mixed + part
        mixed_ref[:, tile] = mixed.astype(bf16)
    mixed = mixed_ref[...]
    for start, block in zip(starts, blocks):
        full_ref[:, pl.ds(start, cols)] = dot_nt(mixed, block[:cols, qkv_width:])
    keep_ref[...] = full_ref[: rows // 2, :]
    send_ref[...] = full_ref[rows // 2 :, :].astype(bf16)


def attend_backward_kernel(
    count, cols, q_width, offset_ref, d_ref, q_ref, kv_ref, cos_ref, sin_ref, mask_ref, *refs
):
    blocks = listed(refs, count)
    keep_ref, send_ref, d_qkv_ref, full_ref = refs[-4:]
    rows = d_ref.shape[0]
    kv_width = LANES
    qkv_width = q_width + 2 * kv_width
    scale = HEAD ** (-0.5)
    starts = [pl.multiple_of(offset_ref[j], cols) for j in range(count)]
    d_mixed = None
    for start, block in zip(starts, blocks):
        part = dot(d_ref[:, pl.ds(start, cols)], block[:cols, qkv_width:])
        d_mixed = part if d_mixed is None else d_mixed + part
    d_mixed = d_mixed.astype(bf16)
    cosine, sine, mask = cos_ref[...], sin_ref[...], mask_ref[...]

    def turned_back(tile):
        return tile * cosine - swapped_halves(tile) * sine

    key_variants = head_variants(kv_ref[:, :kv_width].astype(f32))
    value_variants = head_variants(kv_ref[:, kv_width:].astype(f32))
    tiles = q_width // LANES
    d_keys = [[None, None], [None, None]]
    d_values = [[None, None], [None, None]]
    for i in range(tiles):
        kv_head = i * 2 // tiles
        tile = slice(i * LANES, (i + 1) * LANES)
        q_tile = q_ref[:, tile]
        d_tile = d_mixed[:, tile]
        dq = None
        for side in range(2):
            scores = dot_nt(q_tile, key_variants[kv_head][side]) * scale + mask
            probs = softmax_rows(scores)
            d_probs = dot_nt(d_tile, value_variants[kv_head][side])
            delta = jnp.sum(probs * d_probs, axis=-1, keepdims=True)
            d_scores = (probs * (d_probs - delta)).astype(bf16)
            part = dot(d_scores, key_variants[kv_head][side])
            dq = part if dq is None else dq + part
            for store, lhs, rhs in ((d_keys, d_scores, q_tile), (d_values, probs.astype(bf16), d_tile)):
                part = dot_tn(lhs, rhs)
                before = store[kv_head][side]
                store[kv_head][side] = part if before is None else before + part
        d_qkv_ref[:, tile] = turned_back(dq * scale).astype(bf16)
    lane = lax.broadcasted_iota(jnp.int32, (rows, LANES), 1)

    def merged(store):
        heads = []
        for kv_head in range(2):
            low, high = store[kv_head]
            heads.append((low, high))
        first = heads[0][0] + pltpu.roll(heads[0][1], HEAD, 1)
        second = pltpu.roll(heads[1][0], HEAD, 1) + heads[1][1]
        return jnp.where(lane < HEAD, first, second)

    d_qkv_ref[:, q_width : q_width + kv_width] = turned_back(merged(d_keys) * scale).astype(bf16)
    d_qkv_ref[:, q_width + kv_width :] = merged(d_values).astype(bf16)
    d_qkv = d_qkv_ref[...]
    for start, block in zip(starts, blocks):
        full_ref[:, pl.ds(start, cols)] = dot_nt(d_qkv, block[:cols, :qkv_width])
    keep_ref[...] = full_ref[: rows // 2, :]
    send_ref[...] = full_ref[rows // 2 :, :].astype(bf16)


SMEM = pl.BlockSpec(memory_space=pltpu.SMEM)
VMEM = pl.BlockSpec(memory_space=pltpu.VMEM)
ANYWHERE = pl.BlockSpec(memory_space=pl.ANY)


def call(kernel, out_shape, specs, operands, pins, flops, scratch=(), out_specs=None, grid=(), aliases=None):
    pins = list(pins)
    moved = sum(a.size * a.dtype.itemsize for a in list(operands) + list(out_shape))
    return pl.pallas_call(
        kernel,
        grid=grid,
        out_shape=tuple(out_shape),
        in_specs=list(specs) + [ANYWHERE] * len(pins),
        out_specs=tuple(out_specs or [VMEM] * len(out_shape)),
        scratch_shapes=list(scratch),
        input_output_aliases=aliases or {},
        compiler_params=pltpu.CompilerParams(vmem_limit_bytes=VMEM_BYTES),
        cost_estimate=pl.CostEstimate(flops=flops, bytes_accessed=moved, transcendentals=0),
    )(*operands, *pins)


def attend_forward(offsets, x, tables, blocks, q_width, cols, pins=()):
    rows, width = x.shape
    count = offsets.shape[0]
    out_shape = (
        jax.ShapeDtypeStruct((rows // 2, width), f32),
        jax.ShapeDtypeStruct((rows // 2, width), bf16),
        jax.ShapeDtypeStruct((rows, q_width), bf16),
        jax.ShapeDtypeStruct((rows, 2 * LANES), bf16),
        jax.ShapeDtypeStruct((rows, q_width), bf16),
        jax.ShapeDtypeStruct((rows // 4, width), bf16),
        jax.ShapeDtypeStruct((2, width), f32),
    )
    return call(
        lambda *refs: attend_forward_kernel(count, cols, q_width, *refs),
        out_shape,
        [SMEM] + [VMEM] * (4 + len(blocks)),
        (offsets, x, *tables, *blocks),
        pins,
        2 * rows * width * blocks[0].shape[-1],
        [pltpu.VMEM((rows, width), bf16), pltpu.VMEM((rows, width), f32)],
    )


def attend_backward(offsets, d_attn, q_rot, kv, tables, blocks, cols, pins=()):
    rows, width = d_attn.shape
    q_width = q_rot.shape[1]
    count = offsets.shape[0]
    out_shape = (
        jax.ShapeDtypeStruct((rows // 2, width), f32),
        jax.ShapeDtypeStruct((rows // 2, width), bf16),
        jax.ShapeDtypeStruct((rows, q_width + 2 * LANES), bf16),
    )
    return call(
        lambda *refs: attend_backward_kernel(count, cols, q_width, *refs),
        out_shape,
        [SMEM] + [VMEM] * (6 + len(blocks)),
        (offsets, d_attn, q_rot, kv, *tables, *blocks),
        pins,
        2 * rows * width * blocks[0].shape[-1],
        [pltpu.VMEM((rows, width), f32)],
    )


def weight_views(refs, packed):
    if packed:
        return [[[ref.at[j, i] for j in range(ref.shape[0])] for i in range(3)] for ref in refs[:2]]
    return [[[refs[3 * half + i]] for i in range(3)] for half in range(2)]


def sliced_dot(x_ref, blocks, contract):
    total, start = None, 0
    for block in blocks:
        cols = block.shape[0] if contract is dot else block.shape[1]
        part = contract(x_ref[:, start : start + cols], block[...])
        total = part if total is None else total + part
        start += cols
    return total


def store_parts(outs, start, value):
    rows = value.shape[0] // 4
    for i, out_ref in enumerate(outs):
        part = value[i * rows : (i + 1) * rows]
        out_ref[:, start : start + value.shape[1]] = part.astype(out_ref.dtype)


def mlp_forward_kernel(packed, x_ref, *refs):
    views = weight_views(refs, packed)
    gate_ref, up_ref, hidden_ref = refs[-7:-4]
    units = gate_ref.shape[1] // 2
    hiddens = []
    for half, (gate_w, up_w, _) in enumerate(views):
        gate, up = sliced_dot(x_ref, gate_w, dot), sliced_dot(x_ref, up_w, dot)
        hiddens.append((gate * jax.nn.sigmoid(gate) * up).astype(bf16))
        place = slice(half * units, (half + 1) * units)
        gate_ref[:, place] = gate
        up_ref[:, place] = up
        hidden_ref[:, place] = hiddens[-1]
    start = 0
    for first, second in zip(views[0][2], views[1][2]):
        store_parts(refs[-4:], start, dot(hiddens[0], first[...]) + dot(hiddens[1], second[...]))
        start += first.shape[1]


def mlp_down_kernel(packed, rows, offset_ref, *refs):
    hiddens = refs[:GROUPS]
    views = weight_views(refs[GROUPS:], packed)
    out_ref = refs[-1]
    place = 0
    for hidden_ref in hiddens:
        hidden = hidden_ref[...]
        units = hidden.shape[1] // 2
        count = hidden.shape[0] // rows
        starts = [pl.multiple_of(offset_ref[place + i], rows) for i in range(count)]
        place += count
        start = 0
        for first, second in zip(views[0][2], views[1][2]):
            part = dot(hidden[:, :units], first[...]) + dot(hidden[:, units:], second[...])
            part = part.astype(bf16)
            for i in range(count):
                out_ref[pl.ds(starts[i], rows), start : start + part.shape[1]] = part[
                    i * rows : (i + 1) * rows
                ]
            start += part.shape[1]


def mlp_backward_kernel(packed, again, d_ref, *refs):
    given = refs[: 1 if again else 2]
    views = weight_views(refs[len(given) :], packed)
    d_gate_ref, d_up_ref = refs[-6:-4]
    units = d_gate_ref.shape[1] // 2
    d_gates, d_ups = [], []
    for half, (gate_w, up_w, down_w) in enumerate(views):
        place = slice(half * units, (half + 1) * units)
        d_hidden = sliced_dot(d_ref, down_w, dot_nt)
        if again:
            gate, up = sliced_dot(given[0], gate_w, dot), sliced_dot(given[0], up_w, dot)
            refs[-7][:, place] = (gate * jax.nn.sigmoid(gate) * up).astype(bf16)
        else:
            gate, up = given[0][:, place], given[1][:, place]
        gated = jax.nn.sigmoid(gate)
        d_ups.append((d_hidden * gate * gated).astype(bf16))
        d_gates.append((d_hidden * up * gated * (1.0 + gate * (1.0 - gated))).astype(bf16))
        d_gate_ref[:, place] = d_gates[-1]
        d_up_ref[:, place] = d_ups[-1]
    start = 0
    for blocks in zip(*views[0][:2], *views[1][:2]):
        total = None
        for value, block in zip((d_gates[0], d_ups[0], d_gates[1], d_ups[1]), blocks):
            part = dot_nt(value, block[...])
            total = part if total is None else total + part
        store_parts(refs[-4:], start, total)
        start += total.shape[1]


def weight_specs(layer, mats):
    specs = []
    for m in mats:
        if len(m.shape) == 4:
            specs.append(pl.BlockSpec((m.shape[0] // 2,) + m.shape[1:], lambda i: (layer, 0, 0, 0)))
        else:
            specs.append(pl.BlockSpec((None,) + m.shape[1:], lambda i: (layer, 0, 0)))
    return specs


def part_shapes(rows, width):
    return [jax.ShapeDtypeStruct((rows // 4, width), f32)] + [
        jax.ShapeDtypeStruct((rows // 4, width), bf16)
    ] * 3


def mlp_forward(layer, tokens, mats, units, pins=()):
    rows, width = tokens.shape
    out_shape = [
        jax.ShapeDtypeStruct((rows, 2 * units), f32),
        jax.ShapeDtypeStruct((rows, 2 * units), f32),
        jax.ShapeDtypeStruct((rows, 2 * units), bf16),
    ] + part_shapes(rows, width)
    return call(
        lambda *refs: mlp_forward_kernel(len(mats) == 2, *refs),
        out_shape,
        [VMEM] + weight_specs(layer, mats),
        (tokens, *mats),
        pins,
        12 * rows * width * units,
        grid=(1,),
    )


def mlp_down(layer, offsets, hiddens, mats, width, pins=()):
    rows = sum(h.shape[0] for h in hiddens)
    own = rows // offsets.shape[0]
    return call(
        lambda *refs: mlp_down_kernel(len(mats) == 2, own, *refs),
        [jax.ShapeDtypeStruct((rows, width), bf16)],
        [SMEM] + [VMEM] * len(hiddens) + weight_specs(layer, mats),
        (offsets * own, *hiddens, *mats),
        pins,
        2 * rows * width * hiddens[0].shape[1],
        grid=(1,),
    )[0]


def mlp_backward(layer, d_tokens, given, mats, units, again, pins=()):
    rows, width = d_tokens.shape
    out_shape = [jax.ShapeDtypeStruct((rows, 2 * units), bf16)] * (3 if again else 2)
    out_shape += part_shapes(rows, width)
    return call(
        lambda *refs: mlp_backward_kernel(len(mats) == 2, again, *refs),
        out_shape,
        [VMEM] * (1 + len(given)) + weight_specs(layer, mats),
        (d_tokens, *given, *mats),
        pins,
        (20 if again else 12) * rows * width * units,
        grid=(1,),
    )


def unit_grads_kernel(groups, *refs):
    outs = refs[-2:]
    units = refs[2].shape[1] // 2
    for half, out_ref in enumerate(outs):
        place = slice(half * units, (half + 1) * units)
        totals = [None, None, None]
        for g in range(groups):
            x_ref, d_ref, d_gate_ref, d_up_ref, hidden_ref = refs[g * 5 : g * 5 + 5]
            x, d = x_ref[...], d_ref[...]
            parts = (
                dot_tn(x, d_gate_ref[:, place]),
                dot_tn(x, d_up_ref[:, place]),
                dot_tn(hidden_ref[:, place], d),
            )
            totals = [p if t is None else t + p for t, p in zip(totals, parts)]
        for i in range(3):
            out_ref[0, i] = totals[i].astype(bf16)


def unit_grads(n, inputs, pins=()):
    rows, width = inputs[0][0].shape
    units = inputs[0][2].shape[1] // 2
    cols = width // n
    if cols % LANES:
        made = []
        for place in (slice(0, units), slice(units, 2 * units)):
            totals = [0.0, 0.0, 0.0]
            for x, d, d_gate, d_up, hidden in inputs:
                totals[0] += dot_tn(x, d_gate[:, place]).reshape(n, cols, units)
                totals[1] += dot_tn(x, d_up[:, place]).reshape(n, cols, units)
                totals[2] += dot_tn(hidden[:, place], d).reshape(units, n, cols).transpose(1, 0, 2)
            made.append(jnp.stack(totals, axis=1).astype(bf16))
        return made
    specs, operands = [], []
    for group in inputs:
        for place, array in enumerate(group):
            operands.append(array)
            if place < 2:
                specs.append(pl.BlockSpec((rows, cols), lambda j: (0, j)))
            else:
                specs.append(pl.BlockSpec(array.shape, lambda j: (0, 0)))
    return call(
        lambda *refs: unit_grads_kernel(len(inputs), *refs),
        [jax.ShapeDtypeStruct((n, 3, cols, units), bf16)] * 2,
        specs,
        operands,
        pins,
        12 * len(inputs) * rows * width * units,
        out_specs=[pl.BlockSpec((1, 3, cols, units), lambda j: (j, 0, 0, 0))] * 2,
        grid=(n,),
    )


def add_kernel(kept_ref, got_ref, *refs):
    refs[-1][...] = (kept_ref[...].astype(f32) + got_ref[...].astype(f32)).astype(bf16)


def core_sum(layer, kept, got, into, pins=()):
    n = kept.shape[0]
    if kept.shape[3] % LANES:
        made = (kept.astype(f32) + got.astype(f32)).astype(bf16)
        return made if into is None else jnp.concatenate([made, into], axis=0)
    block = (n // 2,) + kept.shape[1:]
    return call(
        add_kernel,
        [jax.ShapeDtypeStruct((2 * n,) + kept.shape[1:], bf16)],
        [pl.BlockSpec(block, lambda j: (j, 0, 0, 0))] * 2,
        (kept, got),
        ([] if into is None else [into]) + list(pins),
        0,
        out_specs=[pl.BlockSpec(block, lambda j: (2 * layer + j, 0, 0, 0))],
        grid=(2,),
        aliases={} if into is None else {2: 0},
    )[0]


def pack_kernel(gate_ref, up_ref, down_ref, *refs):
    out_ref = refs[-1]
    _, _, cols, units = out_ref.shape
    for i in range(out_ref.shape[0]):
        place = slice(i * units, (i + 1) * units)
        out_ref[i, 0] = gate_ref[:, place]
        out_ref[i, 1] = up_ref[:, place]
        out_ref[i, 2] = down_ref[place, :]


def unpack_kernel(in_ref, *refs):
    gate_ref, up_ref, down_ref = refs[-3:]
    _, _, cols, units = in_ref.shape
    for i in range(in_ref.shape[0]):
        place = slice(i * units, (i + 1) * units)
        gate_ref[:, place] = in_ref[i, 0].astype(f32)
        up_ref[:, place] = in_ref[i, 1].astype(f32)
        down_ref[place, :] = in_ref[i, 2].astype(f32)


def packing_specs(cols, units, steps):
    rows = pl.BlockSpec((cols, steps * units), lambda i: (0, i))
    columns = pl.BlockSpec((steps * units, cols), lambda i: (i, 0))
    packed = pl.BlockSpec((steps, 3, cols, units), lambda i: (i, 0, 0, 0))
    return [rows, rows, columns], packed


def packed_units(gate, up, down, pieces, pins):
    cols, units = gate.shape[0], gate.shape[1] // pieces
    specs, packed = packing_specs(cols, units, 4)
    return call(
        pack_kernel,
        [jax.ShapeDtypeStruct((pieces, 3, cols, units), gate.dtype)],
        specs,
        (gate, up, down),
        pins,
        0,
        out_specs=[packed],
        grid=(pieces // 4,),
    )[0]


def unpacked_units(packed_array, pins):
    pieces, _, cols, units = packed_array.shape
    specs, packed = packing_specs(cols, units, 4)
    return call(
        unpack_kernel,
        [
            jax.ShapeDtypeStruct((cols, pieces * units), f32),
            jax.ShapeDtypeStruct((cols, pieces * units), f32),
            jax.ShapeDtypeStruct((pieces * units, cols), f32),
        ],
        [packed],
        (packed_array,),
        pins,
        0,
        out_specs=specs,
        grid=(pieces // 4,),
    )


def on_device(
    tokens, cotangent, attn_gain, w_query, w_key, w_value, w_out, mlp_gain, w_gate, w_up, w_down
):
    plane = lax.axis_index("pipe")
    core = lax.axis_index("tensor")
    place = lax.axis_index("dp")
    n = lax.axis_size("dp")
    first = plane == 0
    seq_len, width = tokens.shape
    own_cols = width // n
    own = seq_len // 4
    q_width = w_query.shape[2] // 2
    kv_width = w_key.shape[2] // 2
    starts = [
        (2 * c + p) * own
        for c, p in ((core, plane), (core, 1 - plane), (1 - core, plane), (1 - core, 1 - plane))
    ]

    def own_rows(rows):
        return lax.dynamic_slice_in_dim(rows, starts[0], own, 0)

    def relative(rows):
        return jnp.concatenate(
            [lax.dynamic_slice_in_dim(rows, start, own, 0) for start in starts], axis=0
        )

    def natural(rows):
        out = jnp.zeros_like(rows)
        for i, start in enumerate(starts):
            out = lax.dynamic_update_slice_in_dim(out, rows[i * own : (i + 1) * own], start, 0)
        return out

    def halves(matrix, axis):
        return jnp.split(matrix, 2, axis=axis)

    units = w_gate.shape[2] // (2 * n)
    by_blocks = own_cols % LANES == 0 and units == own_cols and n == 8
    block_cols = own_cols if by_blocks else width
    gains = jnp.concatenate([attn_gain, mlp_gain], axis=0)
    packed = [
        jnp.concatenate([q, k, v, o.T], axis=1)
        for q, k, v, o in zip(
            halves(w_query[0], 1), halves(w_key[0], 1), halves(w_value[0], 1), halves(w_out[0], 0)
        )
    ]
    if by_blocks:
        row = jnp.pad(gains.reshape(1, -1), ((0, 15), (0, packed[0].shape[1] - 2 * own_cols)))
        packed = [jnp.concatenate([part, row], axis=0) for part in packed]
    got = to_plane(jnp.where(first, packed[1], packed[0]))
    local = [jnp.where(first, packed[0], got), jnp.where(first, got, packed[1])]
    own_cot = own_rows(cotangent)
    cot_all = gather_tokens(own_cot)
    both = ("pipe", "dp")

    if by_blocks:
        attn_blocks = [[lax.all_gather(block, "dp", axis=0)] for block in local]
        offsets = jnp.arange(n, dtype=jnp.int32) * own_cols
        packed_weights = packed_units(w_gate[0], w_up[0], w_down[0], 2 * n, [got] + cot_all)
        mats = [lax.all_to_all(packed_weights, both, 0, 0, tiled=True)]
    else:
        other_gains = to_plane(gains)
        local_gains = [jnp.where(first, gains, other_gains), jnp.where(first, other_gains, gains)]
        attn_blocks = [
            [
                lax.all_gather(block, "dp", axis=0, tiled=True),
                lax.all_gather(gain, "dp", axis=1, tiled=True),
            ]
            for block, gain in zip(local, local_gains)
        ]
        offsets = jnp.zeros((1,), jnp.int32)
        down_both = lax.all_to_all(w_down[0], both, 0, 0, tiled=True).reshape(2, n, units, own_cols)
        mats = [
            lax.all_to_all(w_gate[0], both, 1, 0, tiled=True).reshape(2, width, units),
            lax.all_to_all(w_up[0], both, 1, 0, tiled=True).reshape(2, width, units),
            down_both.transpose(0, 2, 1, 3).reshape(2, units, width),
        ]
    mats = mats + [to_core(m) for m in mats]

    positions = jnp.concatenate([start + jnp.arange(own, dtype=jnp.int32) for start in starts])
    causal = positions[None, :] <= positions[:, None]
    tables = rope_tables(positions) + (jnp.where(causal, 0.0, -1e30).astype(f32),)

    def attention(layer, layer_in):
        keep, send, q_rot, kv, mixed, xn_own, gains = attend_forward(
            offsets, layer_in, tables, attn_blocks[layer], q_width, block_cols
        )
        middle = layer_in[:own].astype(f32) + sum_four(keep, send)
        xn_two = gather_tokens(normed(middle, gains[1:2]).astype(bf16))
        return xn_two, middle, (gains, xn_own, q_rot, kv, mixed)

    def d_attention(layer, d_middle, layer_in, kept, pins=()):
        gains, xn_own, q_rot, kv, mixed = kept
        keep, send, d_qkv = attend_backward(
            offsets,
            gather_four(d_middle.astype(bf16)),
            q_rot,
            kv,
            tables,
            attn_blocks[layer],
            block_cols,
            pins,
        )
        d_xn_one = sum_four(keep, send)
        _, norm_pull = jax.vjp(normed, layer_in[:own].astype(f32), gains[0:1])
        d_in_norm, d_gain_one = norm_pull(d_xn_one)
        return d_middle + d_in_norm, d_qkv, d_gain_one

    def d_norm(upstream, d_xn_two, middle, gains):
        _, norm_pull = jax.vjp(normed, middle, gains[1:2])
        d_mid_norm, d_gain_two = norm_pull(d_xn_two)
        return upstream.astype(f32) + d_mid_norm, d_gain_two

    def grad_inputs(xs, d_tokens, d_units, hiddens):
        return [
            (x, d, du[0], du[1], h) for x, d, du, h in zip(xs, d_tokens, d_units, hiddens)
        ]

    def dp_all(block, axis):
        return lax.all_gather(block, "dp", axis=axis, tiled=True)

    in_first = relative(tokens)
    xn_first, middle_first, kept_first = attention(0, in_first)
    units_first = [mlp_forward(0, x, mats, units) for x in xn_first]
    first_out = (middle_first + sum_tokens([r[3:] for r in units_first])).astype(bf16)
    in_second = gather_four(first_out)
    xn_second, middle_second, kept_second = attention(1, in_second)
    units_second = [
        mlp_backward(1, d, [x], mats, units, True) for d, x in zip(cot_all, xn_second)
    ]
    hidden_second = [r[0] for r in units_second]
    d_units_second = [r[1:] for r in units_second]
    d_middle_second, d_mlp_gain_second = d_norm(
        own_cot, sum_tokens([d[2:] for d in d_units_second]), middle_second, kept_second[0]
    )
    mixed_all = dp_all(jnp.stack([kept_first[4], kept_second[4]]), 1)
    d_second, d_qkv_second, d_attn_gain_second = d_attention(
        1, d_middle_second, in_second, kept_second
    )
    d_second = d_second.astype(bf16)
    d_qkv_second_all = dp_all(d_qkv_second, 0)
    d_all = gather_tokens(d_second)
    made, sent = unit_grads(
        n, grad_inputs(xn_second, cot_all, d_units_second, hidden_second), [d_second]
    )
    packed_grads = core_sum(1, made, to_core(sent), None)
    owners = jnp.stack(
        [
            (place ^ (2 * k + j % 2)) * 2 + (plane ^ (j // 2))
            for group in column_groups()
            for j in range(4)
            for k in group
        ]
    )
    partial = mlp_down(1, owners, hidden_second, mats, width, [d_middle_second])
    partial = lax.psum_scatter(partial, ("dp", "pipe"), scatter_dimension=0, tiled=True)
    second_out = (middle_second + partial.astype(f32)).astype(bf16)
    d_units_first = [
        mlp_backward(0, d, r[:2], mats, units, False, [mixed_all])
        for d, r in zip(d_all, units_first)
    ]
    made, sent = unit_grads(
        n, grad_inputs(xn_first, d_all, d_units_first, [r[2] for r in units_first])
    )
    d_middle_first, d_mlp_gain_first = d_norm(
        d_second, sum_tokens([d[2:] for d in d_units_first]), middle_first, kept_first[0]
    )
    packed_grads = core_sum(0, made, to_core(sent), packed_grads, [d_middle_first])
    d_first, d_qkv_first, d_attn_gain_first = d_attention(
        0, d_middle_first, in_first, kept_first, [d_qkv_second_all]
    )
    gain_rows = jnp.concatenate(
        [d_attn_gain_first, d_mlp_gain_first, d_attn_gain_second, d_mlp_gain_second]
    ).astype(bf16)
    pad_rows = -(-gain_rows.size // (16 * d_qkv_first.shape[1])) * 16
    gain_rows = jnp.pad(
        gain_rows.reshape(-1), (0, pad_rows * d_qkv_first.shape[1] - gain_rows.size)
    ).reshape(pad_rows, -1)
    gathered = lax.all_gather(jnp.concatenate([d_qkv_first, gain_rows]), "dp", axis=0)
    d_qkv_first_all = gathered[:, :seq_len].reshape(n * seq_len, -1)
    gain_sums = jnp.sum(gathered[:, seq_len:].astype(f32), axis=0).reshape(-1)
    gain_sums = gain_sums[: 4 * width].reshape(4, width)
    gain_sums = gain_sums + to_core(gain_sums)
    gain_sums = gain_sums + to_plane(gain_sums)

    columns = jnp.stack(
        [kept_first[1], d_middle_first.astype(bf16), kept_second[1], d_middle_second.astype(bf16)]
    )
    columns = lax.all_to_all(columns.reshape(4 * own, n, own_cols), "dp", 1, 0)
    columns = gather_four(columns.reshape(1, n, 4, own, own_cols))
    columns = columns.transpose(2, 1, 0, 3, 4).reshape(4, n * seq_len, own_cols)

    def attention_grads(layer, d_qkv_all):
        return jnp.concatenate(
            [
                dot_tn(columns[2 * layer], d_qkv_all),
                dot_tn(columns[2 * layer + 1], mixed_all[layer]),
            ],
            axis=1,
        ).astype(bf16)

    small_first = attention_grads(0, d_qkv_first_all)
    small_second = attention_grads(1, d_qkv_second_all)
    small_own = jnp.where(first, small_first, small_second)
    small_got = to_plane(jnp.where(first, small_second, small_first))
    small = [
        jnp.where(first, small_own, small_got).astype(f32),
        jnp.where(first, small_got, small_own).astype(f32),
    ]

    def joined(start, size):
        return jnp.concatenate([part[:, start : start + size] for part in small], axis=1)

    grad_query = joined(0, q_width)
    grad_key = joined(q_width, kv_width)
    grad_value = joined(q_width + kv_width, kv_width)
    grad_out = joined(q_width + 2 * kv_width, q_width).T
    packed_grads = lax.all_to_all(packed_grads, both, 0, 0, tiled=True)
    if by_blocks:
        grad_gate, grad_up, grad_down = unpacked_units(packed_grads, [small_got, gain_sums, second_out])
    else:
        parts = [packed_grads[:, i].astype(f32) for i in range(3)]
        grad_gate, grad_up = [part.transpose(1, 0, 2).reshape(own_cols, -1) for part in parts[:2]]
        grad_down = parts[2].reshape(-1, own_cols)
    gain_sums = jnp.where(first, gain_sums[:2], gain_sums[2:])
    gain_grads = lax.dynamic_slice_in_dim(gain_sums, place * own_cols, own_cols, 1)

    activations = natural(jnp.where(first, in_second, gather_four(second_out)))
    input_grads = natural(
        jnp.where(first, gather_four(d_first), gather_four(d_second).astype(f32))
    )
    return (
        activations[None],
        input_grads[None],
        gain_grads[0][None],
        grad_query[None],
        grad_key[None],
        grad_value[None],
        grad_out[None],
        gain_grads[1][None],
        grad_gate[None],
        grad_up[None],
        grad_down[None],
    )


def solution(mesh):
    token_spec = P("dp", None)
    gain_spec = P("pipe", "dp")
    row_spec = P("pipe", "dp", "tensor")
    col_spec = P("pipe", "tensor", "dp")
    in_specs = (
        token_spec,
        token_spec,
        gain_spec,
        row_spec,
        row_spec,
        row_spec,
        col_spec,
        gain_spec,
        row_spec,
        row_spec,
        col_spec,
    )
    out_specs = (
        P("pipe", "dp", None),
        P("pipe", "dp", None),
        gain_spec,
        row_spec,
        row_spec,
        row_spec,
        col_spec,
        gain_spec,
        row_spec,
        row_spec,
        col_spec,
    )
    return jax.shard_map(
        on_device, mesh=mesh, in_specs=in_specs, out_specs=out_specs, check_vma=False
    )
```

time: 2590 us -> 884 us (0.34)
  waiting for transfers between devices: 1920 us -> 518 us
  matrix products: 295 us -> 2.12 us
  local copies, waits for them, and re-layouts: 189 us -> 21.4 us
  starting transfers between devices: 12.3 us -> 174 us
  Pallas kernels: 0 us -> 117 us
  other arithmetic: 100 us -> 31.1 us
  blocking collectives: 40.5 us -> 0 us
    reduce_scatter x1, waiting for transfers between devices: 946 us -> 0.01 us  [on_device(): lax.psum_scatter(partial, ('dp', 'pipe'), scatter_dimension=0, tiled=True)]
    all_gather x7 -> x5, waiting for transfers between devices: 849 us -> 61.2 us  [the longest x1 61.2 us: on_device(): lax.all_gather(jnp.concatenate([d_qkv_first, gain_rows]), 'dp', axis=0)]
    dot_general x67 -> x4, matrix products: 295 us -> 2.12 us  [dot_tn(): lax.dot_general(a, b, (((0,), (0,)), ((), ())), preferred_element_type=f32)]
    ppermute x4 -> x92, waiting for transfers between devices: 10.7 us -> 248 us  [the longest x28 150 us: to_plane(): return lax.ppermute(block, 'pipe', [(0, 1), (1, 0)])]
    all_to_all x0 -> x3, waiting for transfers between devices: none -> 208 us  [the longest x1 199 us: on_device(): mats = [lax.all_to_all(packed_weights, both, 0, 0, tiled=True)]]
    ppermute x4 -> x92, starting transfers between devices: 11.3 us -> 157 us  [the longest x35 99.9 us: to_dp(): lax.ppermute(block, 'dp', [(i, i ^ flip) for i in range(lax.axis_size('dp...]
    pallas_call x0 -> x17, Pallas kernels: none -> 117 us  [call(): pl.pallas_call(kernel, grid=grid, out_shape=tuple(out_shape), in_specs=li...]
    psum x11 -> x0, waiting for transfers between devices: 113 us -> none  [the longest x3 29.9 us: on_device(): lax.psum(d_xn_one.astype(jnp.bfloat16), 'tensor').astype(jnp.float32)]
  transfers between devices with their start and end apart: 23 -> 101, of which waited for: 21 -> 50; matrix products, arithmetic and copies ran while one was open for 6% -> 5% of each run, Pallas kernels for 0% -> 11%
where the time goes in v1:
time: 884 us; the launch traced here: 880 us
  waiting for transfers between devices  518 us (59%)
  starting transfers between devices  174 us (20%)
  Pallas kernels  117 us (13%)
  other arithmetic  31.1 us (4%)
  local copies, waits for them, and re-layouts  21.4 us (2%)
  between operations  15.9 us (2%)
    all_to_all x1, waiting for transfers between devices, on_device(): mats = [lax.all_to_all(packed_weights, both, 0, 0, tiled=True)]  199 us
    ppermute x28, waiting for transfers between devices, to_plane(): return lax.ppermute(block, 'pipe', [(0, 1), (1, 0)])  150 us
    pallas_call x17, Pallas kernels, call(): pl.pallas_call(kernel, grid=grid, out_shape=tuple(out_shape), in_specs=li...  117 us
    ppermute x35, starting transfers between devices, to_dp(): lax.ppermute(block, 'dp', [(i, i ^ flip) for i in range(lax.axis_size('dp...  99.9 us
    ppermute x35, waiting for transfers between devices, to_dp(): lax.ppermute(block, 'dp', [(i, i ^ flip) for i in range(lax.axis_size('dp...  74.6 us
    all_gather x1, waiting for transfers between devices, on_device(): lax.all_gather(jnp.concatenate([d_qkv_first, gain_rows]), 'dp', axis=0)  61.2 us
    ppermute x28, starting transfers between devices, to_plane(): return lax.ppermute(block, 'pipe', [(0, 1), (1, 0)])  38.7 us
  transfers between devices with their start and end apart: 101, of which 50 were waited for; matrix products, arithmetic and copies ran while one was open for 5% of the time, Pallas kernels for 11%

profile of v1, /device:TPU:0, one launch (start us, length us, event | category | flops | bytes accessed | tf_op | source)
XLA Modules:
  0.0 879.7 jit_solution(15299393850909632171)
XLA Ops:
  28.9 11.6 %collective-permute-done.9 = bf16[64,2048]{1,0:T(8,128)(2,1)S(1)} collective-permute-done((bf16[64,2048]{1,0:T(8,128)(2,1)S(1)}, bf16[64,2048]{1,0:T(8,128)(2,1)S(1)}, u32[]{:S(2)}, u32[]{:S(2)}) %collective-permute-start.9) | collective-permute-done | bytes 262176 | tf_op jit(solution)/shard_map/ppermute | solution.py:50
  72.5 198.7 %all-to-all-done.refs_1_.refs_2_.refs_3_ = bf16[16,3,256,256]{3,2,1,0:T(8,128)(2,1)} async-done(((bf16[16,3,256,256]{3,2,1,0:T(8,128)(2,1)}), bf16[16,3,256,256]{3,2,1,0:T(8,128)(2,1)}, u32[]{:S(2)}, u32[]{:S(2)}) %all-to-all-start) | async-done | bytes 6291488 | tf_op jit(solution)/shard_map/all_to_all | solution.py:664
  275.9 7.0 shard_map.194
  292.6 22.8 %collective-permute-start.21 = (bf16[32,2048]{1,0:T(8,128)(2,1)S(1)}, bf16[32,2048]{1,0:T(8,128)(2,1)S(1)}, u32[]{:S(2)}, u32[]{:S(2)}) collective-permute-start(bf16[32,2048]{1,0:T(8,128)(2,1)S(1)} %get-tuple-element.227), channel_id=1, source_target_pairs={{0,8},{2,10},{4,12},{6,14},{8,0},{10,2},{12,4},{14,6},{1,9},{3,11}... | collective-permute-start | bytes 393224 | tf_op jit(solution)/shard_map/ppermute | solution.py:54
  320.4 11.8 %collective-permute-done.21 = bf16[32,2048]{1,0:T(8,128)(2,1)S(1)} collective-permute-done((bf16[32,2048]{1,0:T(8,128)(2,1)S(1)}, bf16[32,2048]{1,0:T(8,128)(2,1)S(1)}, u32[]{:S(2)}, u32[]{:S(2)}) %collective-permute-start.21) | collective-permute-done | bytes 131104 | tf_op jit(solution)/shard_map/ppermute | solution.py:54
  337.6 9.0 %collective-permute-done.23 = bf16[64,2048]{1,0:T(8,128)(2,1)S(1)} collective-permute-done((bf16[64,2048]{1,0:T(8,128)(2,1)S(1)}, bf16[64,2048]{1,0:T(8,128)(2,1)S(1)}, u32[]{:S(2)}, u32[]{:S(2)}) %collective-permute-start.23) | collective-permute-done | bytes 262176 | tf_op jit(solution)/shard_map/ppermute | solution.py:54
  380.9 10.1 %collective-permute-start.29 = (bf16[32,2048]{1,0:T(8,128)(2,1)S(1)}, bf16[32,2048]{1,0:T(8,128)(2,1)S(1)}, u32[]{:S(2)}, u32[]{:S(2)}) collective-permute-start(bf16[32,2048]{1,0:T(8,128)(2,1)S(1)} %get-tuple-element.259), channel_id=1, source_target_pairs={{0,8},{2,10},{4,12},{6,14},{8,0},{10,2},{12,4},{14,6},{1,9},{3,11}... | collective-permute-start | bytes 393224 | tf_op jit(solution)/shard_map/ppermute | solution.py:54
  406.3 7.0 shard_map.198
  448.4 10.8 %collective-permute-done.42 = bf16[64,2048]{1,0:T(8,128)(2,1)S(1)} collective-permute-done((bf16[64,2048]{1,0:T(8,128)(2,1)S(1)}, bf16[64,2048]{1,0:T(8,128)(2,1)S(1)}, u32[]{:S(2)}, u32[]{:S(2)}) %collective-permute-start.42) | collective-permute-done | bytes 262176 | tf_op jit(solution)/shard_map/ppermute | solution.py:50
  463.8 7.5 shard_map.200
  475.9 7.5 shard_map.199
  511.6 8.0 shard_map.202
  534.9 9.3 %shard_map.207 = (bf16[8,3,256,256]{3,2,1,0:T(8,128)(2,1)}, bf16[8,3,256,256]{3,2,1,0:T(8,128)(2,1)}) custom-call(bf16[256,2048]{1,0:T(8,128)(2,1)} %copy-done.13, bf16[256,2048]{1,0:T(8,128)(2,1)} %copy-done.2, bf16[256,512]{1,0:T(8,128)(2,1)} %get-tuple-element.136.refs_2_, bf16[256,512]{1,0:T(8,128)(2,1)} %get-tuple-element.137.refs_3_, ...), custom_call_target="tpu_custom_call" | custom-call | flops 3221225472 | bytes 12058624 | tf_op jit(solution)/shard_map/pallas_call | solution.py:258
  562.4 13.2 %collective-permute-done.60 = bf16[64,2048]{1,0:T(8,128)(2,1)S(1)} collective-permute-done((bf16[64,2048]{1,0:T(8,128)(2,1)S(1)}, bf16[64,2048]{1,0:T(8,128)(2,1)S(1)}, u32[]{:S(2)}, u32[]{:S(2)}) %collective-permute-start.60) | collective-permute-done | bytes 262176 | tf_op jit(solution)/shard_map/ppermute | solution.py:54
  575.7 6.9 shard_map.204
  594.1 9.4 %shard_map.206 = (bf16[8,3,256,256]{3,2,1,0:T(8,128)(2,1)}, bf16[8,3,256,256]{3,2,1,0:T(8,128)(2,1)}) custom-call(bf16[256,2048]{1,0:T(8,128)(2,1)} %copy-done.17, bf16[256,2048]{1,0:T(8,128)(2,1)} %copy-done.15, bf16[256,512]{1,0:T(8,128)(2,1)} %get-tuple-element.128.refs_2_, bf16[256,512]{1,0:T(8,128)(2,1)} %get-tuple-element.129.refs_3_, ...), custom_call_target="tpu_custom_call" | custom-call | flops 3221225472 | bytes 12058624 | tf_op jit(solution)/shard_map/pallas_call | solution.py:258
  609.9 9.0 %collective-permute-start.75 = (bf16[32,2048]{1,0:T(8,128)(2,1)S(1)}, bf16[32,2048]{1,0:T(8,128)(2,1)S(1)}, u32[]{:S(2)}, u32[]{:S(2)}) collective-permute-start(bf16[32,2048]{1,0:T(8,128)(2,1)S(1)} %get-tuple-element.255), channel_id=1, source_target_pairs={{0,8},{2,10},{4,12},{6,14},{8,0},{10,2},{12,4},{14,6},{1,9},{3,11}... | collective-permute-start | bytes 393224 | tf_op jit(solution)/shard_map/ppermute | solution.py:54
  635.5 8.1 shard_map.205
  659.9 8.9 %all-to-all-done.1 = bf16[1,128,8,256]{3,1,0,2:T(8,128)(2,1)S(1)} async-done(((bf16[1,128,8,256]{3,1,0,2:T(8,128)(2,1)}), bf16[1,128,8,256]{3,1,0,2:T(8,128)(2,1)S(1)}, u32[]{:S(2)}, u32[]{:S(2)}) %all-to-all-start.1) | async-done | bytes 524320 | tf_op jit(solution)/shard_map/all_to_all | solution.py:793
  676.2 74.2 %collective-permute-done.81 = f32[32,2048]{1,0:T(8,128)S(1)} collective-permute-done((f32[32,2048]{1,0:T(8,128)S(1)}, f32[32,2048]{1,0:T(8,128)S(1)}, u32[]{:S(2)}, u32[]{:S(2)}) %collective-permute-start.81) | collective-permute-done | bytes 262176 | tf_op jit(solution)/shard_map/ppermute | solution.py:50
  755.6 8.6 collective-permute-done.53
  773.0 61.2 %all-gather.17.cloned.1.call-done = bf16[1152,768]{1,0:T(8,128)(2,1)} async-done(((bf16[144,768]{1,0:T(8,128)(2,1)}), bf16[1152,768]{1,0:T(8,128)(2,1)}) %all-gather.17.cloned.1.call-update) | async-done | bytes 1769488 | tf_op jit(solution)/shard_map/all_gather | solution.py:783
  842.6 13.6 %collective-permute-done.89.refs_0_ = bf16[256,1280]{1,0:T(8,128)(2,1)S(1)} collective-permute-done((bf16[256,1280]{1,0:T(8,128)(2,1)S(1)}, bf16[256,1280]{1,0:T(8,128)(2,1)S(1)}, u32[]{:S(2)}, u32[]{:S(2)}) %collective-permute-start.89) | collective-permute-done | bytes 655392 | tf_op jit(solution)/shard_map/ppermute | solution.py:50
  864.9 7.7 shard_map.210
  (479 shorter events, 322.2 us)
Async XLA Ops:
  16.3 40.3 %collective-permute-start = (bf16[272,1280]{1,0:T(8,128)(2,1)S(1)}, bf16[272,1280]{1,0:T(8,128)(2,1)S(1)}, u32[]{:S(2)}, u32[]{:S(2)}) collective-permute-start(bf16[272,1280]{1,0:T(8,128)(2,1)S(1)} %broadcast_select_fusion.2), channel_id=1, source_target_pairs={{0,16},{16,0},{1,17},{17,1},{2,18},{18,2},{3,19},{19,3},{4,20},{20... | collective-permute-start | bytes 2088968 | tf_op jit(solution)/shard_map/ppermute | solution.py:50
  24.3 23.0 %collective-permute-start.10 = (bf16[64,2048]{1,0:T(8,128)(2,1)S(1)}, bf16[64,2048]{1,0:T(8,128)(2,1)S(1)}, u32[]{:S(2)}, u32[]{:S(2)}) collective-permute-start(bf16[64,2048]{1,0:T(8,128)(2,1)S(1)} %pad_maximum_fusion.12), channel_id=1, source_target_pairs={{0,18},{2,16},{4,22},{6,20},{8,26},{10,24},{12,30},{14,28},{16,2},... | collective-permute-start | bytes 786440 | tf_op jit(solution)/shard_map/ppermute | solution.py:60
  28.3 23.5 %collective-permute-start.14 = (bf16[64,2048]{1,0:T(8,128)(2,1)S(1)}, bf16[64,2048]{1,0:T(8,128)(2,1)S(1)}, u32[]{:S(2)}, u32[]{:S(2)}) collective-permute-start(bf16[64,2048]{1,0:T(8,128)(2,1)S(1)} %get-tuple-element.271), channel_id=1, source_target_pairs={{0,16},{16,0},{1,17},{17,1},{2,18},{18,2},{3,19},{19,3},{4,20},{20... | collective-permute-start | bytes 786440 | tf_op jit(solution)/shard_map/ppermute | solution.py:50
  63.7 207.6 %all-to-all-start = ((bf16[16,3,256,256]{3,2,1,0:T(8,128)(2,1)}), bf16[16,3,256,256]{3,2,1,0:T(8,128)(2,1)}, u32[]{:S(2)}, u32[]{:S(2)}) async-start(bf16[16,3,256,256]{3,2,1,0:T(8,128)(2,1)} %shard_map.195), calls=%async_computation | async-start | bytes 12582912 | tf_op jit(solution)/shard_map/all_to_all | solution.py:664
  69.7 206.2 %all-gather.13.cloned.1.call-start = ((), (), s32[]{:S(2)}) async-start(), calls=%async_computation.7 | async-start | bytes 6266880 | tf_op jit(solution)/shard_map/all_gather | solution.py:661
  71.2 335.1 %all-gather.15.cloned.1.call-start = ((), (), s32[]{:S(2)}) async-start(), calls=%async_computation.8 | async-start | bytes 6266880 | tf_op jit(solution)/shard_map/all_gather | solution.py:661
  71.9 503.8 %all-gather.9.cloned.1.call-start = ((), (), s32[]{:S(2)}) async-start(), calls=%async_computation.5 | async-start | bytes 2359296 | tf_op jit(solution)/shard_map/all_gather | solution.py:724
  271.2 84.6 %collective-permute-start.16 = (bf16[16,3,256,256]{3,2,1,0:T(8,128)(2,1)}, bf16[16,3,256,256]{3,2,1,0:T(8,128)(2,1)}, u32[]{:S(2)}, u32[]{:S(2)}) collective-permute-start(bf16[16,3,256,256]{3,2,1,0:T(8,128)(2,1)} %all-to-all-done.refs_1_.refs_2_.refs_3_), channel_id=1, source_target_pairs={{0,1},{1,0},{2,3},{3,2},{4,5},{5,4},{6,7},{7,6},{8,9},{9,8},{10,11... | collective-permute-start | bytes 18874376 | tf_op jit(solution)/shard_map/ppermute | solution.py:46
  292.6 39.6 %collective-permute-start.21 = (bf16[32,2048]{1,0:T(8,128)(2,1)S(1)}, bf16[32,2048]{1,0:T(8,128)(2,1)S(1)}, u32[]{:S(2)}, u32[]{:S(2)}) collective-permute-start(bf16[32,2048]{1,0:T(8,128)(2,1)S(1)} %get-tuple-element.227), channel_id=1, source_target_pairs={{0,8},{2,10},{4,12},{6,14},{8,0},{10,2},{12,4},{14,6},{1,9},{3,11}... | collective-permute-start | bytes 393224 | tf_op jit(solution)/shard_map/ppermute | solution.py:54
  427.0 208.5 %all-gather.11.cloned.1.call-start = ((), (), s32[]{:S(2)}) async-start(), calls=%async_computation.6 | async-start | bytes 1769472 | tf_op jit(solution)/shard_map/all_gather | solution.py:724
  439.0 34.4 %collective-permute-start.36 = (bf16[64,2048]{1,0:T(8,128)(2,1)S(1)}, bf16[64,2048]{1,0:T(8,128)(2,1)S(1)}, u32[]{:S(2)}, u32[]{:S(2)}) collective-permute-start(bf16[64,2048]{1,0:T(8,128)(2,1)S(1)} %pad_maximum_fusion.14), channel_id=1, source_target_pairs={{0,2},{2,0},{4,6},{6,4},{8,10},{10,8},{12,14},{14,12},{1,3},{3,1},... | collective-permute-start | bytes 786440 | tf_op jit(solution)/shard_map/ppermute | solution.py:54
  439.5 35.3 %collective-permute-start.37 = (bf16[64,2048]{1,0:T(8,128)(2,1)S(1)}, bf16[64,2048]{1,0:T(8,128)(2,1)S(1)}, u32[]{:S(2)}, u32[]{:S(2)}) collective-permute-start(bf16[64,2048]{1,0:T(8,128)(2,1)S(1)} %pad_maximum_fusion.14), channel_id=1, source_target_pairs={{0,16},{16,0},{1,17},{17,1},{2,18},{18,2},{3,19},{19,3},{4,20},{20... | collective-permute-start | bytes 786440 | tf_op jit(solution)/shard_map/ppermute | solution.py:50
  441.2 33.7 %collective-permute-start.38 = (bf16[64,2048]{1,0:T(8,128)(2,1)S(1)}, bf16[64,2048]{1,0:T(8,128)(2,1)S(1)}, u32[]{:S(2)}, u32[]{:S(2)}) collective-permute-start(bf16[64,2048]{1,0:T(8,128)(2,1)S(1)} %pad_maximum_fusion.14), channel_id=1, source_target_pairs={{0,18},{2,16},{4,22},{6,20},{8,26},{10,24},{12,30},{14,28},{16,2},... | collective-permute-start | bytes 786440 | tf_op jit(solution)/shard_map/ppermute | solution.py:60
  524.6 226.6 %reduce-scatter.2.cloned.1.call-start = ((), (), s32[]{:S(2)}) async-start(), calls=%async_computation.4 | async-start | bytes 2228224 | tf_op jit(solution)/shard_map/reduce_scatter | solution.py:760
  544.2 107.0 %collective-permute-start.91 = (bf16[8,3,256,256]{3,2,1,0:T(8,128)(2,1)}, bf16[8,3,256,256]{3,2,1,0:T(8,128)(2,1)}, u32[]{:S(2)}, u32[]{:S(2)}) collective-permute-start(bf16[8,3,256,256]{3,2,1,0:T(8,128)(2,1)} %get-tuple-element.141), channel_id=1, source_target_pairs={{0,1},{1,0},{2,3},{3,2},{4,5},{5,4},{6,7},{7,6},{8,9},{9,8},{10,11... | collective-permute-start | bytes 9437192 | tf_op jit(solution)/shard_map/ppermute | solution.py:46
  550.4 25.1 %collective-permute-start.60 = (bf16[64,2048]{1,0:T(8,128)(2,1)S(1)}, bf16[64,2048]{1,0:T(8,128)(2,1)S(1)}, u32[]{:S(2)}, u32[]{:S(2)}) collective-permute-start(bf16[64,2048]{1,0:T(8,128)(2,1)S(1)} %get-tuple-element.262), channel_id=1, source_target_pairs={{0,2},{2,0},{4,6},{6,4},{8,10},{10,8},{12,14},{14,12},{1,3},{3,1},... | collective-permute-start | bytes 786440 | tf_op jit(solution)/shard_map/ppermute | solution.py:54
  605.7 49.9 %collective-permute-start.90 = (bf16[8,3,256,256]{3,2,1,0:T(8,128)(2,1)}, bf16[8,3,256,256]{3,2,1,0:T(8,128)(2,1)}, u32[]{:S(2)}, u32[]{:S(2)}) collective-permute-start(bf16[8,3,256,256]{3,2,1,0:T(8,128)(2,1)} %get-tuple-element.135), channel_id=1, source_target_pairs={{0,1},{1,0},{2,3},{3,2},{4,5},{5,4},{6,7},{7,6},{8,9},{9,8},{10,11... | collective-permute-start | bytes 9437192 | tf_op jit(solution)/shard_map/ppermute | solution.py:46
  644.8 24.0 %all-to-all-start.1 = ((bf16[1,128,8,256]{3,1,0,2:T(8,128)(2,1)}), bf16[1,128,8,256]{3,1,0,2:T(8,128)(2,1)S(1)}, u32[]{:S(2)}, u32[]{:S(2)}) async-start(bf16[1,128,8,256]{3,1,0,2:T(8,128)(2,1)} %copy.48), calls=%async_computation.2 | async-start | bytes 1048576 | tf_op jit(solution)/shard_map/all_to_all | solution.py:793
  649.7 23.9 %collective-permute-start.80 = (bf16[32,2048]{1,0:T(8,128)(2,1)S(1)}, bf16[32,2048]{1,0:T(8,128)(2,1)S(1)}, u32[]{:S(2)}, u32[]{:S(2)}) collective-permute-start(bf16[32,2048]{1,0:T(8,128)(2,1)S(1)} %slice.362), channel_id=1, source_target_pairs={{0,16},{16,0},{1,17},{17,1},{2,18},{18,2},{3,19},{19,3},{4,20},{20... | collective-permute-start | bytes 393224 | tf_op jit(solution)/shard_map/ppermute | solution.py:50
  668.8 196.1 %all-to-all-start.2 = ((bf16[16,3,256,256]{3,2,1,0:T(8,128)(2,1)}), bf16[16,3,256,256]{3,2,1,0:T(8,128)(2,1)}, u32[]{:S(2)}, u32[]{:S(2)}) async-start(bf16[16,3,256,256]{3,2,1,0:T(8,128)(2,1)} %shard_map.209), calls=%async_computation.3 | async-start | bytes 12582912 | tf_op jit(solution)/shard_map/all_to_all | solution.py:822
  673.5 160.7 %all-gather.17.cloned.1.call-start = ((), (), s32[]{:S(2)}) async-start(), calls=%async_computation.9 | async-start | bytes 1990656 | tf_op jit(solution)/shard_map/all_gather | solution.py:783
  673.9 76.5 %collective-permute-start.81 = (f32[32,2048]{1,0:T(8,128)S(1)}, f32[32,2048]{1,0:T(8,128)S(1)}, u32[]{:S(2)}, u32[]{:S(2)}) collective-permute-start(f32[32,2048]{1,0:T(8,128)S(1)} %fusion.7), channel_id=1, source_target_pairs={{0,16},{16,0},{1,17},{17,1},{2,18},{18,2},{3,19},{19,3},{4,20},{20... | collective-permute-start | bytes 786440 | tf_op jit(solution)/shard_map/ppermute | solution.py:50
  675.8 89.1 %collective-permute-start.84 = (bf16[64,2048]{1,0:T(8,128)(2,1)S(1)}, bf16[64,2048]{1,0:T(8,128)(2,1)}, u32[]{:S(2)}, u32[]{:S(2)}) collective-permute-start(bf16[64,2048]{1,0:T(8,128)(2,1)S(1)} %get-tuple-element.261), channel_id=1, source_target_pairs={{0,1},{1,0},{2,3},{3,2},{4,5},{5,4},{6,7},{7,6},{8,9},{9,8},{10,11... | collective-permute-start | bytes 786440 | tf_op jit(solution)/shard_map/ppermute | solution.py:46
  675.9 88.3 %collective-permute-start.87 = (bf16[1,8,4,32,256]{4,3,2,1,0:T(8,128)(2,1)S(1)}, bf16[1,8,4,32,256]{4,3,2,1,0:T(8,128)(2,1)S(1)}, u32[]{:S(2)}, u32[]{:S(2)}) collective-permute-start(bf16[1,8,4,32,256]{4,3,2,1,0:T(8,128)(2,1)S(1)} %bitcast.126), channel_id=1, source_target_pairs={{0,16},{16,0},{1,17},{17,1},{2,18},{18,2},{3,19},{19,3},{4,20},{20... | collective-permute-start | bytes 1572872 | tf_op jit(solution)/shard_map/ppermute | solution.py:50
  (130 other events, 1587.3 us)
Sparse Core Ops, SparseCore 0:
  73.3 177.3 all-gather.12
  253.5 106.3 all-gather.14
  427.1 66.2 all-gather.8
  524.7 65.4 all-gather.10
  625.5 122.0 reduce-scatter.1
  755.7 78.4 all-gather.16

commit v2 on v1

--- a/solution.py
+++ b/solution.py
@@ -268,6 +268,19 @@
     )(*operands, *pins)
 
 
+def after(array, pins):
+    return call(
+        lambda *refs: None,
+        [jax.ShapeDtypeStruct(array.shape, array.dtype)],
+        [ANYWHERE],
+        (array,),
+        pins,
+        0,
+        out_specs=[ANYWHERE],
+        aliases={0: 0},
+    )[0]
+
+
 def attend_forward(offsets, x, tables, blocks, q_width, cols, pins=()):
     rows, width = x.shape
     count = offsets.shape[0]
@@ -374,18 +387,15 @@
             start += part.shape[1]
 
 
-def mlp_backward_kernel(packed, again, d_ref, *refs):
-    given = refs[: 1 if again else 2]
-    views = weight_views(refs[len(given) :], packed)
-    d_gate_ref, d_up_ref = refs[-6:-4]
-    units = d_gate_ref.shape[1] // 2
+def d_mlp_core(views, d_ref, given, units, outs, hidden_ref):
+    d_gate_ref, d_up_ref = outs[:2]
     d_gates, d_ups = [], []
     for half, (gate_w, up_w, down_w) in enumerate(views):
         place = slice(half * units, (half + 1) * units)
         d_hidden = sliced_dot(d_ref, down_w, dot_nt)
-        if again:
+        if hidden_ref is not None:
             gate, up = sliced_dot(given[0], gate_w, dot), sliced_dot(given[0], up_w, dot)
-            refs[-7][:, place] = (gate * jax.nn.sigmoid(gate) * up).astype(bf16)
+            hidden_ref[:, place] = (gate * jax.nn.sigmoid(gate) * up).astype(bf16)
         else:
             gate, up = given[0][:, place], given[1][:, place]
         gated = jax.nn.sigmoid(gate)
@@ -399,8 +409,24 @@
         for value, block in zip((d_gates[0], d_ups[0], d_gates[1], d_ups[1]), blocks):
             part = dot_nt(value, block[...])
             total = part if total is None else total + part
-        store_parts(refs[-4:], start, total)
+        store_parts(outs[2:], start, total)
         start += total.shape[1]
+
+
+def mlp_backward_kernel(packed, d_ref, gate_ref, up_ref, *refs):
+    outs = refs[-6:]
+    units = outs[0].shape[1] // 2
+    d_mlp_core(weight_views(refs, packed), d_ref, (gate_ref, up_ref), units, outs, None)
+
+
+def mlp_both_kernel(packed, rows, offset_ref, all_ref, x_ref, *refs):
+    sorted_ref, hidden_ref = refs[-8:-6]
+    outs = refs[-6:]
+    units = outs[0].shape[1] // 2
+    for i in range(sorted_ref.shape[0] // rows):
+        start = pl.multiple_of(offset_ref[i], rows)
+        sorted_ref[i * rows : (i + 1) * rows, :] = all_ref[pl.ds(start, rows), :]
+    d_mlp_core(weight_views(refs, packed), sorted_ref, (x_ref,), units, outs, hidden_ref)
 
 
 def weight_specs(layer, mats):
@@ -451,17 +477,31 @@
     )[0]
 
 
-def mlp_backward(layer, d_tokens, given, mats, units, again, pins=()):
+def mlp_backward(layer, d_tokens, gate, up, mats, units, pins=()):
     rows, width = d_tokens.shape
-    out_shape = [jax.ShapeDtypeStruct((rows, 2 * units), bf16)] * (3 if again else 2)
-    out_shape += part_shapes(rows, width)
-    return call(
-        lambda *refs: mlp_backward_kernel(len(mats) == 2, again, *refs),
+    out_shape = [jax.ShapeDtypeStruct((rows, 2 * units), bf16)] * 2 + part_shapes(rows, width)
+    return call(
+        lambda *refs: mlp_backward_kernel(len(mats) == 2, *refs),
         out_shape,
-        [VMEM] * (1 + len(given)) + weight_specs(layer, mats),
-        (d_tokens, *given, *mats),
+        [VMEM] * 3 + weight_specs(layer, mats),
+        (d_tokens, gate, up, *mats),
         pins,
-        (20 if again else 12) * rows * width * units,
+        12 * rows * width * units,
+        grid=(1,),
+    )
+
+
+def mlp_both(layer, offsets, d_all, tokens, mats, units, own, pins=()):
+    rows, width = tokens.shape
+    out_shape = [jax.ShapeDtypeStruct((rows, width), bf16)]
+    out_shape += [jax.ShapeDtypeStruct((rows, 2 * units), bf16)] * 3 + part_shapes(rows, width)
+    return call(
+        lambda *refs: mlp_both_kernel(len(mats) == 2, own, *refs),
+        out_shape,
+        [SMEM, VMEM, VMEM] + weight_specs(layer, mats),
+        (offsets * own, d_all, tokens, *mats),
+        pins,
+        20 * rows * width * units,
         grid=(1,),
     )
 
@@ -552,14 +592,27 @@
         out_ref[i, 2] = down_ref[place, :]
 
 
-def unpack_kernel(in_ref, *refs):
-    gate_ref, up_ref, down_ref = refs[-3:]
+def unpack_kernel(in_ref, gate_w_ref, up_w_ref, *refs):
+    gate_ref, up_ref, down_ref, sums_ref = refs[-4:]
     _, _, cols, units = in_ref.shape
+    total = jnp.zeros(sums_ref.shape, f32)
     for i in range(in_ref.shape[0]):
         place = slice(i * units, (i + 1) * units)
-        gate_ref[:, place] = in_ref[i, 0].astype(f32)
-        up_ref[:, place] = in_ref[i, 1].astype(f32)
+        gate, up = in_ref[i, 0].astype(f32), in_ref[i, 1].astype(f32)
+        gate_ref[:, place] = gate
+        up_ref[:, place] = up
         down_ref[place, :] = in_ref[i, 2].astype(f32)
+        both = gate_w_ref[:, place].astype(f32) * gate + up_w_ref[:, place].astype(f32) * up
+        for lane in range(0, units, LANES):
+            total = total + both[:, lane : lane + LANES]
+
+    @pl.when(pl.program_id(0) == 0)
+    def _():
+        sums_ref[...] = total
+
+    @pl.when(pl.program_id(0) > 0)
+    def _():
+        sums_ref[...] += total
 
 
 def packing_specs(cols, units, steps):
@@ -584,7 +637,7 @@
     )[0]
 
 
-def unpacked_units(packed_array, pins):
+def unpacked_units(packed_array, gate_w, up_w, pins):
     pieces, _, cols, units = packed_array.shape
     specs, packed = packing_specs(cols, units, 4)
     return call(
@@ -593,12 +646,13 @@
             jax.ShapeDtypeStruct((cols, pieces * units), f32),
             jax.ShapeDtypeStruct((cols, pieces * units), f32),
             jax.ShapeDtypeStruct((pieces * units, cols), f32),
+            jax.ShapeDtypeStruct((cols, LANES), f32),
         ],
-        [packed],
-        (packed_array,),
+        [packed] + specs[:2],
+        (packed_array, gate_w, up_w),
         pins,
         0,
-        out_specs=specs,
+        out_specs=specs + [pl.BlockSpec((cols, LANES), lambda i: (0, 0))],
         grid=(pieces // 4,),
     )
 
@@ -654,13 +708,27 @@
     got = to_plane(jnp.where(first, packed[1], packed[0]))
     local = [jnp.where(first, packed[0], got), jnp.where(first, got, packed[1])]
     own_cot = own_rows(cotangent)
-    cot_all = gather_tokens(own_cot)
+    cot_all = lax.all_gather(own_cot, ("dp", "pipe"), axis=0, tiled=True)
+    owners = [
+        jnp.stack(
+            [
+                (place ^ (2 * k + j % 2)) * 2 + (plane ^ (j // 2))
+                for j in range(4)
+                for k in group
+            ]
+        )
+        for group in column_groups()
+    ]
     both = ("pipe", "dp")
 
     if by_blocks:
-        attn_blocks = [[lax.all_gather(block, "dp", axis=0)] for block in local]
+        attn_blocks = [
+            [lax.all_gather(after(local[0], [cot_all]), "dp", axis=0)],
+            [lax.all_gather(local[1], "dp", axis=0)],
+        ]
         offsets = jnp.arange(n, dtype=jnp.int32) * own_cols
-        packed_weights = packed_units(w_gate[0], w_up[0], w_down[0], 2 * n, [got] + cot_all)
+        packed_weights = packed_units(w_gate[0], w_up[0], w_down[0], 2 * n, [])
+        packed_weights = after(packed_weights, local)
         mats = [lax.all_to_all(packed_weights, both, 0, 0, tiled=True)]
     else:
         other_gains = to_plane(gains)
@@ -685,9 +753,9 @@
     causal = positions[None, :] <= positions[:, None]
     tables = rope_tables(positions) + (jnp.where(causal, 0.0, -1e30).astype(f32),)
 
-    def attention(layer, layer_in):
+    def attention(layer, layer_in, pins=()):
         keep, send, q_rot, kv, mixed, xn_own, gains = attend_forward(
-            offsets, layer_in, tables, attn_blocks[layer], q_width, block_cols
+            offsets, layer_in, tables, attn_blocks[layer], q_width, block_cols, pins
         )
         middle = layer_in[:own].astype(f32) + sum_four(keep, send)
         xn_two = gather_tokens(normed(middle, gains[1:2]).astype(bf16))
@@ -706,14 +774,12 @@
             pins,
         )
         d_xn_one = sum_four(keep, send)
-        _, norm_pull = jax.vjp(normed, layer_in[:own].astype(f32), gains[0:1])
-        d_in_norm, d_gain_one = norm_pull(d_xn_one)
-        return d_middle + d_in_norm, d_qkv, d_gain_one
+        _, norm_pull = jax.vjp(lambda v: normed(v, gains[0:1]), layer_in[:own].astype(f32))
+        return d_middle + norm_pull(d_xn_one)[0], d_qkv
 
     def d_norm(upstream, d_xn_two, middle, gains):
-        _, norm_pull = jax.vjp(normed, middle, gains[1:2])
-        d_mid_norm, d_gain_two = norm_pull(d_xn_two)
-        return upstream.astype(f32) + d_mid_norm, d_gain_two
+        _, norm_pull = jax.vjp(lambda v: normed(v, gains[1:2]), middle)
+        return upstream.astype(f32) + norm_pull(d_xn_two)[0]
 
     def grad_inputs(xs, d_tokens, d_units, hiddens):
         return [
@@ -730,88 +796,82 @@
     in_second = gather_four(first_out)
     xn_second, middle_second, kept_second = attention(1, in_second)
     units_second = [
-        mlp_backward(1, d, [x], mats, units, True) for d, x in zip(cot_all, xn_second)
+        mlp_both(1, owner, cot_all, x, mats, units, own) for owner, x in zip(owners, xn_second)
     ]
-    hidden_second = [r[0] for r in units_second]
-    d_units_second = [r[1:] for r in units_second]
-    d_middle_second, d_mlp_gain_second = d_norm(
+    cot_sorted = [r[0] for r in units_second]
+    hidden_second = [r[1] for r in units_second]
+    d_units_second = [r[2:] for r in units_second]
+    d_middle_second = d_norm(
         own_cot, sum_tokens([d[2:] for d in d_units_second]), middle_second, kept_second[0]
     )
     mixed_all = dp_all(jnp.stack([kept_first[4], kept_second[4]]), 1)
-    d_second, d_qkv_second, d_attn_gain_second = d_attention(
-        1, d_middle_second, in_second, kept_second
+    d_second, d_qkv_second = d_attention(
+        1, d_middle_second, in_second, kept_second, [mixed_all]
     )
     d_second = d_second.astype(bf16)
     d_qkv_second_all = dp_all(d_qkv_second, 0)
     d_all = gather_tokens(d_second)
     made, sent = unit_grads(
-        n, grad_inputs(xn_second, cot_all, d_units_second, hidden_second), [d_second]
+        n, grad_inputs(xn_second, cot_sorted, d_units_second, hidden_second), [d_second]
     )
     packed_grads = core_sum(1, made, to_core(sent), None)
-    owners = jnp.stack(
-        [
-            (place ^ (2 * k + j % 2)) * 2 + (plane ^ (j // 2))
-            for group in column_groups()
-            for j in range(4)
-            for k in group
-        ]
-    )
-    partial = mlp_down(1, owners, hidden_second, mats, width, [d_middle_second])
-    partial = lax.psum_scatter(partial, ("dp", "pipe"), scatter_dimension=0, tiled=True)
+    relative_owners = [
+        (j // 2) * n + (place ^ (2 * k + j % 2))
+        for group in column_groups()
+        for j in range(4)
+        for k in group
+    ]
+    partial = mlp_down(1, jnp.stack(relative_owners), hidden_second, mats, width, [d_second])
+    half = partial.shape[0] // 2
+    partial = partial[:half].astype(f32) + to_plane(partial[half:]).astype(f32)
+    partial = lax.psum_scatter(partial.astype(bf16), "dp", scatter_dimension=0, tiled=True)
     second_out = (middle_second + partial.astype(f32)).astype(bf16)
     d_units_first = [
-        mlp_backward(0, d, r[:2], mats, units, False, [mixed_all])
+        mlp_backward(0, d, *r[:2], mats, units, [d_qkv_second_all, packed_grads])
         for d, r in zip(d_all, units_first)
     ]
     made, sent = unit_grads(
         n, grad_inputs(xn_first, d_all, d_units_first, [r[2] for r in units_first])
     )
-    d_middle_first, d_mlp_gain_first = d_norm(
+    d_middle_first = d_norm(
         d_second, sum_tokens([d[2:] for d in d_units_first]), middle_first, kept_first[0]
     )
     packed_grads = core_sum(0, made, to_core(sent), packed_grads, [d_middle_first])
-    d_first, d_qkv_first, d_attn_gain_first = d_attention(
-        0, d_middle_first, in_first, kept_first, [d_qkv_second_all]
-    )
-    gain_rows = jnp.concatenate(
-        [d_attn_gain_first, d_mlp_gain_first, d_attn_gain_second, d_mlp_gain_second]
-    ).astype(bf16)
-    pad_rows = -(-gain_rows.size // (16 * d_qkv_first.shape[1])) * 16
-    gain_rows = jnp.pad(
-        gain_rows.reshape(-1), (0, pad_rows * d_qkv_first.shape[1] - gain_rows.size)
-    ).reshape(pad_rows, -1)
-    gathered = lax.all_gather(jnp.concatenate([d_qkv_first, gain_rows]), "dp", axis=0)
-    d_qkv_first_all = gathered[:, :seq_len].reshape(n * seq_len, -1)
-    gain_sums = jnp.sum(gathered[:, seq_len:].astype(f32), axis=0).reshape(-1)
-    gain_sums = gain_sums[: 4 * width].reshape(4, width)
-    gain_sums = gain_sums + to_core(gain_sums)
-    gain_sums = gain_sums + to_plane(gain_sums)
-
-    columns = jnp.stack(
+    def column_rows(blocks):
+        count = len(blocks)
+        rows = jnp.concatenate(blocks).reshape(count * own, n, own_cols)
+        return lax.all_to_all(rows, "dp", 1, 0).reshape(1, n, count, own, own_cols)
+
+    def all_rows(columns):
+        rows = gather_four(columns).transpose(2, 1, 0, 3, 4)
+        return rows.reshape(rows.shape[0], n * seq_len, own_cols)
+
+    columns = column_rows(
         [kept_first[1], d_middle_first.astype(bf16), kept_second[1], d_middle_second.astype(bf16)]
     )
-    columns = lax.all_to_all(columns.reshape(4 * own, n, own_cols), "dp", 1, 0)
-    columns = gather_four(columns.reshape(1, n, 4, own, own_cols))
-    columns = columns.transpose(2, 1, 0, 3, 4).reshape(4, n * seq_len, own_cols)
-
-    def attention_grads(layer, d_qkv_all):
+    d_first, d_qkv_first = d_attention(
+        0, d_middle_first, in_first, kept_first, [columns, partial]
+    )
+    d_qkv_all = [dp_all(d_qkv_first, 0), d_qkv_second_all]
+    columns = all_rows(after(columns, [d_qkv_first]))
+
+    def attention_grads(layer, d_qkv):
         return jnp.concatenate(
             [
-                dot_tn(columns[2 * layer], d_qkv_all),
+                dot_tn(columns[2 * layer], d_qkv),
                 dot_tn(columns[2 * layer + 1], mixed_all[layer]),
             ],
             axis=1,
         ).astype(bf16)
 
-    small_first = attention_grads(0, d_qkv_first_all)
-    small_second = attention_grads(1, d_qkv_second_all)
+    small_first = attention_grads(0, d_qkv_all[0])
+    small_second = attention_grads(1, d_qkv_all[1])
     small_own = jnp.where(first, small_first, small_second)
     small_got = to_plane(jnp.where(first, small_second, small_first))
     small = [
         jnp.where(first, small_own, small_got).astype(f32),
         jnp.where(first, small_got, small_own).astype(f32),
     ]
-
     def joined(start, size):
         return jnp.concatenate([part[:, start : start + size] for part in small], axis=1)
 
@@ -819,16 +879,28 @@
     grad_key = joined(q_width, kv_width)
     grad_value = joined(q_width + kv_width, kv_width)
     grad_out = joined(q_width + 2 * kv_width, q_width).T
-    packed_grads = lax.all_to_all(packed_grads, both, 0, 0, tiled=True)
+    packed_grads = lax.all_to_all(
+        packed_grads, both, 0, 0, tiled=True
+    )
     if by_blocks:
-        grad_gate, grad_up, grad_down = unpacked_units(packed_grads, [small_got, gain_sums, second_out])
+        grad_gate, grad_up, grad_down, unit_sums = unpacked_units(
+            packed_grads, w_gate[0], w_up[0], [second_out]
+        )
+        unit_sums = jnp.sum(unit_sums, axis=1)
     else:
         parts = [packed_grads[:, i].astype(f32) for i in range(3)]
         grad_gate, grad_up = [part.transpose(1, 0, 2).reshape(own_cols, -1) for part in parts[:2]]
         grad_down = parts[2].reshape(-1, own_cols)
-    gain_sums = jnp.where(first, gain_sums[:2], gain_sums[2:])
-    gain_grads = lax.dynamic_slice_in_dim(gain_sums, place * own_cols, own_cols, 1)
-
+        unit_sums = jnp.sum(
+            w_gate[0].astype(f32) * grad_gate + w_up[0].astype(f32) * grad_up, axis=1
+        )
+    def row_sums(pairs):
+        return sum(jnp.sum(w[0].astype(f32) * grad, axis=1) for w, grad in pairs)
+
+    attn_sums = row_sums(((w_query, grad_query), (w_key, grad_key), (w_value, grad_value)))
+    gain_sums = jnp.stack([attn_sums, unit_sums])
+    gain_sums = gain_sums + to_core(gain_sums)
+    gain_grads = gain_sums / gains.astype(f32)
     activations = natural(jnp.where(first, in_second, gather_four(second_out)))
     input_grads = natural(
         jnp.where(first, gather_four(d_first), gather_four(d_second).astype(f32))

time: 884 us -> 879 us (level)
  starting transfers between devices: 174 us -> 134 us
  waiting for transfers between devices: 518 us -> 539 us
    all_to_all x1, waiting for transfers between devices: 199 us -> 123 us  [on_device(): mats = [lax.all_to_all(packed_weights, both, 0, 0, tiled=True)]]
    ppermute x28 -> x26, waiting for transfers between devices: 150 us -> 103 us  [to_plane(): return lax.ppermute(block, 'pipe', [(0, 1), (1, 0)])]
    reduce_scatter x1, waiting for transfers between devices: 0.01 us -> 44.2 us  [on_device(): lax.psum_scatter(partial.astype(bf16), 'dp', scatter_dimension=0, tiled=T...]
    all_gather x2 -> x3, waiting for transfers between devices: 0.02 us -> 40.5 us  [dp_all(): return lax.all_gather(block, 'dp', axis=axis, tiled=True)]
    all_gather x3, waiting for transfers between devices: 61.2 us -> 101 us  [the longest x1 84 us: on_device(): cot_all = lax.all_gather(own_cot, ('dp', 'pipe'), axis=0, tiled=True)]
    ppermute x35 -> x30, starting transfers between devices: 99.9 us -> 62.9 us  [to_dp(): lax.ppermute(block, 'dp', [(i, i ^ flip) for i in range(lax.axis_size('dp...]
    ppermute x35 -> x30, waiting for transfers between devices: 74.6 us -> 90.2 us  [to_dp(): lax.ppermute(block, 'dp', [(i, i ^ flip) for i in range(lax.axis_size('dp...]
    pallas_call x17 -> x20, Pallas kernels: 117 us -> 119 us  [call(): pl.pallas_call(kernel, grid=grid, out_shape=tuple(out_shape), in_specs=li...]
  transfers between devices with their start and end apart: 101 -> 93, of which waited for: 50 -> 48; matrix products, arithmetic and copies ran while one was open for 5% -> 5% of each run, Pallas kernels for 11% -> 10%
where the time goes in v2:
time: 879 us; the launch traced here: 868 us
  waiting for transfers between devices  539 us (61%)
  starting transfers between devices  134 us (15%)
  Pallas kernels  119 us (14%)
  other arithmetic  31.8 us (4%)
  local copies, waits for them, and re-layouts  25.2 us (3%)
  between operations  16 us (2%)
    all_to_all x1, waiting for transfers between devices, on_device(): mats = [lax.all_to_all(packed_weights, both, 0, 0, tiled=True)]  123 us
    pallas_call x20, Pallas kernels, call(): pl.pallas_call(kernel, grid=grid, out_shape=tuple(out_shape), in_specs=li...  119 us
    ppermute x26, waiting for transfers between devices, to_plane(): return lax.ppermute(block, 'pipe', [(0, 1), (1, 0)])  103 us
    ppermute x30, waiting for transfers between devices, to_dp(): lax.ppermute(block, 'dp', [(i, i ^ flip) for i in range(lax.axis_size('dp...  90.2 us
    all_gather x1, waiting for transfers between devices, on_device(): cot_all = lax.all_gather(own_cot, ('dp', 'pipe'), axis=0, tiled=True)  84 us
    ppermute x30, starting transfers between devices, to_dp(): lax.ppermute(block, 'dp', [(i, i ^ flip) for i in range(lax.axis_size('dp...  62.9 us
    reduce_scatter x1, waiting for transfers between devices, on_device(): lax.psum_scatter(partial.astype(bf16), 'dp', scatter_dimension=0, tiled=T...  44.2 us
    all_gather x3, waiting for transfers between devices, dp_all(): return lax.all_gather(block, 'dp', axis=axis, tiled=True)  40.5 us
  transfers between devices with their start and end apart: 93, of which 48 were waited for; matrix products, arithmetic and copies ran while one was open for 5% of the time, Pallas kernels for 10%

profile of v2, /device:TPU:0, one launch (start us, length us, event | category | flops | bytes accessed | tf_op | source)
XLA Modules:
  0.0 867.9 jit_solution(3534869188223990934)
XLA Ops:
  19.5 10.7 %collective-permute-done = bf16[272,1280]{1,0:T(8,128)(2,1)S(1)} collective-permute-done((bf16[272,1280]{1,0:T(8,128)(2,1)S(1)}, bf16[272,1280]{1,0:T(8,128)(2,1)S(1)}, u32[]{:S(2)}, u32[]{:S(2)}) %collective-permute-start) | collective-permute-done | bytes 696352 | tf_op jit(solution)/shard_map/ppermute | solution.py:50
  38.9 84.0 %all-gather.9.cloned.1.call-done.refs_1_ = bf16[512,2048]{1,0:T(8,128)(2,1)} async-done(((bf16[32,2048]{1,0:T(8,128)(2,1)}), bf16[512,2048]{1,0:T(8,128)(2,1)}) %all-gather.9.cloned.1.call-update) | async-done | bytes 2097168 | tf_op jit(solution)/shard_map/all_gather | solution.py:711
  123.7 122.7 %all-to-all-done.refs_1_.refs_3_ = bf16[16,3,256,256]{3,2,1,0:T(8,128)(2,1)} async-done(((bf16[16,3,256,256]{3,2,1,0:T(8,128)(2,1)}), bf16[16,3,256,256]{3,2,1,0:T(8,128)(2,1)}, u32[]{:S(2)}, u32[]{:S(2)}) %all-to-all-start) | async-done | bytes 6291488 | tf_op jit(solution)/shard_map/all_to_all | solution.py:732
  250.4 9.8 %all-gather.17.cloned.1.call-done = bf16[2176,1280]{1,0:T(8,128)(2,1)} async-done(((bf16[272,1280]{1,0:T(8,128)(2,1)}), bf16[2176,1280]{1,0:T(8,128)(2,1)}) %all-gather.17.cloned.1.call-update) | async-done | bytes 5570576 | tf_op jit(solution)/shard_map/all_gather | solution.py:726
  284.4 14.0 %collective-permute-done.12 = bf16[32,2048]{1,0:T(8,128)(2,1)S(1)} collective-permute-done((bf16[32,2048]{1,0:T(8,128)(2,1)S(1)}, bf16[32,2048]{1,0:T(8,128)(2,1)S(1)}, u32[]{:S(2)}, u32[]{:S(2)}) %collective-permute-start.12) | collective-permute-done | bytes 131104 | tf_op jit(solution)/shard_map/ppermute | solution.py:54
  314.9 12.1 %collective-permute-done.4 = bf16[64,2048]{1,0:T(8,128)(2,1)S(1)} collective-permute-done((bf16[64,2048]{1,0:T(8,128)(2,1)S(1)}, bf16[64,2048]{1,0:T(8,128)(2,1)S(1)}, u32[]{:S(2)}, u32[]{:S(2)}) %collective-permute-start.4) | collective-permute-done | bytes 262176 | tf_op jit(solution)/shard_map/ppermute | solution.py:54
  347.0 9.5 %collective-permute-done.17 = bf16[64,2048]{1,0:T(8,128)(2,1)S(1)} collective-permute-done((bf16[64,2048]{1,0:T(8,128)(2,1)}, bf16[64,2048]{1,0:T(8,128)(2,1)S(1)}, u32[]{:S(2)}, u32[]{:S(2)}) %collective-permute-start.17) | collective-permute-done | bytes 262176 | tf_op jit(solution)/shard_map/ppermute | solution.py:54
  358.5 13.7 %collective-permute-start.20 = (bf16[32,2048]{1,0:T(8,128)(2,1)S(1)}, bf16[32,2048]{1,0:T(8,128)(2,1)S(1)}, u32[]{:S(2)}, u32[]{:S(2)}) collective-permute-start(bf16[32,2048]{1,0:T(8,128)(2,1)S(1)} %get-tuple-element.249), channel_id=1, source_target_pairs={{0,8},{2,10},{4,12},{6,14},{8,0},{10,2},{12,4},{14,6},{1,9},{3,11}... | collective-permute-start | bytes 393224 | tf_op jit(solution)/shard_map/ppermute | solution.py:54
  443.1 7.7 shard_map.201
  455.5 7.8 shard_map.202
  474.0 9.7 %collective-permute-done.39 = bf16[64,2048]{1,0:T(8,128)(2,1)S(1)} collective-permute-done((bf16[64,2048]{1,0:T(8,128)(2,1)}, bf16[64,2048]{1,0:T(8,128)(2,1)S(1)}, u32[]{:S(2)}, u32[]{:S(2)}) %collective-permute-start.39) | collective-permute-done | bytes 262176 | tf_op jit(solution)/shard_map/ppermute | solution.py:54
  486.2 12.3 %collective-permute-done.42 = bf16[32,2048]{1,0:T(8,128)(2,1)S(1)} collective-permute-done((bf16[32,2048]{1,0:T(8,128)(2,1)S(1)}, bf16[32,2048]{1,0:T(8,128)(2,1)S(1)}, u32[]{:S(2)}, u32[]{:S(2)}) %collective-permute-start.42) | collective-permute-done | bytes 131104 | tf_op jit(solution)/shard_map/ppermute | solution.py:54
  507.2 8.0 shard_map.203
  524.7 9.3 %shard_map.205 = (bf16[8,3,256,256]{3,2,1,0:T(8,128)(2,1)}, bf16[8,3,256,256]{3,2,1,0:T(8,128)(2,1)}) custom-call(bf16[256,2048]{1,0:T(8,128)(2,1)} %copy-done.9, bf16[256,2048]{1,0:T(8,128)(2,1)} %get-tuple-element.114.refs_1_, bf16[256,512]{1,0:T(8,128)(2,1)} %get-tuple-element.115.refs_2_, bf16[256,512]{1,0:T(8,128)(2,1)} %get-tuple-element.116.refs_3_, ...), custom_call_target="tpu_custom_call" | custom-call | flops 3221225472 | bytes 12058624 | tf_op jit(solution)/shard_map/pallas_call | solution.py:258
  561.9 19.2 %collective-permute-done.53 = bf16[64,2048]{1,0:T(8,128)(2,1)S(1)} collective-permute-done((bf16[64,2048]{1,0:T(8,128)(2,1)S(1)}, bf16[64,2048]{1,0:T(8,128)(2,1)S(1)}, u32[]{:S(2)}, u32[]{:S(2)}) %collective-permute-start.53) | collective-permute-done | bytes 262176 | tf_op jit(solution)/shard_map/ppermute | solution.py:50
  630.2 9.3 %shard_map.211 = (bf16[8,3,256,256]{3,2,1,0:T(8,128)(2,1)}, bf16[8,3,256,256]{3,2,1,0:T(8,128)(2,1)}) custom-call(bf16[256,2048]{1,0:T(8,128)(2,1)} %copy-done.12, bf16[256,2048]{1,0:T(8,128)(2,1)} %copy-done.8, bf16[256,512]{1,0:T(8,128)(2,1)} %get-tuple-element.139.refs_2_, bf16[256,512]{1,0:T(8,128)(2,1)} %get-tuple-element.140.refs_3_, ...), custom_call_target="tpu_custom_call" | custom-call | flops 3221225472 | bytes 12058624 | tf_op jit(solution)/shard_map/pallas_call | solution.py:258
  659.0 16.7 %all-to-all-done.1 = bf16[1,128,8,256]{3,1,0,2:T(8,128)(2,1)S(1)} async-done(((bf16[1,128,8,256]{3,1,0,2:T(8,128)(2,1)}), bf16[1,128,8,256]{3,1,0,2:T(8,128)(2,1)S(1)}, u32[]{:S(2)}, u32[]{:S(2)}) %all-to-all-start.1) | async-done | bytes 524320 | tf_op jit(solution)/shard_map/all_to_all | solution.py:843
  681.4 44.2 %reduce-scatter.2.cloned.1.call-done.refs_9_ = bf16[32,2048]{1,0:T(8,128)(2,1)} async-done(((bf16[256,2048]{1,0:T(8,128)(2,1)}), bf16[32,2048]{1,0:T(8,128)(2,1)}) %reduce-scatter.2.cloned.1.call-update) | async-done | bytes 131088 | tf_op jit(solution)/shard_map/reduce_scatter | solution.py:827
  728.1 13.0 %collective-permute-done.49 = bf16[32,2048]{1,0:T(8,128)(2,1)S(1)} collective-permute-done((bf16[32,2048]{1,0:T(8,128)(2,1)S(1)}, bf16[32,2048]{1,0:T(8,128)(2,1)S(1)}, u32[]{:S(2)}, u32[]{:S(2)}) %collective-permute-start.49) | collective-permute-done | bytes 131104 | tf_op jit(solution)/shard_map/ppermute | solution.py:50
  742.8 8.0 shard_map.209
  769.2 9.3 %collective-permute-done.78 = bf16[1,8,4,32,256]{4,3,2,1,0:T(8,128)(2,1)S(1)} collective-permute-done((bf16[1,8,4,32,256]{4,3,2,1,0:T(8,128)(2,1)}, bf16[1,8,4,32,256]{4,3,2,1,0:T(8,128)(2,1)S(1)}, u32[]{:S(2)}, u32[]{:S(2)}) %collective-permute-start.78) | collective-permute-done | bytes 524320 | tf_op jit(solution)/shard_map/ppermute | solution.py:50
  785.9 40.5 %all-gather.15.cloned.1.call-done = bf16[1024,768]{1,0:T(8,128)(2,1)} async-done(((bf16[128,768]{1,0:T(8,128)(2,1)}), bf16[1024,768]{1,0:T(8,128)(2,1)}) %all-gather.15.cloned.1.call-update) | async-done | bytes 1572880 | tf_op jit(solution)/shard_map/all_gather | solution.py:790
  830.7 14.6 %collective-permute-done.80 = bf16[256,1280]{1,0:T(8,128)(2,1)S(1)} collective-permute-done((bf16[256,1280]{1,0:T(8,128)(2,1)S(1)}, bf16[256,1280]{1,0:T(8,128)(2,1)S(1)}, u32[]{:S(2)}, u32[]{:S(2)}) %collective-permute-start.80) | collective-permute-done | bytes 655392 | tf_op jit(solution)/shard_map/ppermute | solution.py:50
  848.5 8.9 %shard_map.213 = (f32[256,4096]{1,0:T(8,128)}, f32[256,4096]{1,0:T(8,128)}, f32[4096,256]{1,0:T(8,128)}, f32[256,128]{1,0:T(8,128)}) custom-call(bf16[16,3,256,256]{3,2,1,0:T(8,128)(2,1)} %all-to-all-done.2.in_ref, bf16[256,4096]{1,0:T(8,128)(2,1)} %bitcast.139, bf16[256,4096]{1,0:T(8,128)(2,1)} %bitcast.141, bf16[32,2048]{1,0:T(8,128)(2,1)} %copy-done.7), custom_call_target="tpu_custom_call" | custom-call | bytes 23199744 | tf_op jit(solution)/shard_map/pallas_call | solution.py:258
  (448 shorter events, 336.9 us)
Async XLA Ops:
  7.2 115.7 %all-gather.9.cloned.1.call-start = ((), (), s32[]{:S(2)}) async-start(), calls=%async_computation.4 | async-start | bytes 2228224 | tf_op jit(solution)/shard_map/all_gather | solution.py:711
  31.6 214.8 %all-to-all-start = ((bf16[16,3,256,256]{3,2,1,0:T(8,128)(2,1)}), bf16[16,3,256,256]{3,2,1,0:T(8,128)(2,1)}, u32[]{:S(2)}, u32[]{:S(2)}) async-start(bf16[16,3,256,256]{3,2,1,0:T(8,128)(2,1)} %shard_map.197), calls=%async_computation | async-start | bytes 12582912 | tf_op jit(solution)/shard_map/all_to_all | solution.py:732
  38.8 221.4 %all-gather.17.cloned.1.call-start = ((), (), s32[]{:S(2)}) async-start(), calls=%async_computation.9 | async-start | bytes 6266880 | tf_op jit(solution)/shard_map/all_gather | solution.py:726
  122.9 278.5 %all-gather.19.cloned.1.call-start = ((), (), s32[]{:S(2)}) async-start(), calls=%async_computation.10 | async-start | bytes 6266880 | tf_op jit(solution)/shard_map/all_gather | solution.py:727
  123.6 383.6 %all-gather.11.cloned.1.call-start = ((), (), s32[]{:S(2)}) async-start(), calls=%async_computation.5 | async-start | bytes 2359296 | tf_op jit(solution)/shard_map/all_gather | solution.py:790
  246.4 80.7 %collective-permute-start.7 = (bf16[16,3,256,256]{3,2,1,0:T(8,128)(2,1)}, bf16[16,3,256,256]{3,2,1,0:T(8,128)(2,1)}, u32[]{:S(2)}, u32[]{:S(2)}) collective-permute-start(bf16[16,3,256,256]{3,2,1,0:T(8,128)(2,1)} %all-to-all-done.refs_1_.refs_3_), channel_id=1, source_target_pairs={{0,1},{1,0},{2,3},{3,2},{4,5},{5,4},{6,7},{7,6},{8,9},{9,8},{10,11... | collective-permute-start | bytes 18874376 | tf_op jit(solution)/shard_map/ppermute | solution.py:46
  302.0 25.0 %collective-permute-start.4 = (bf16[64,2048]{1,0:T(8,128)(2,1)S(1)}, bf16[64,2048]{1,0:T(8,128)(2,1)S(1)}, u32[]{:S(2)}, u32[]{:S(2)}) collective-permute-start(bf16[64,2048]{1,0:T(8,128)(2,1)S(1)} %pad_maximum_fusion.12), channel_id=1, source_target_pairs={{0,2},{2,0},{4,6},{6,4},{8,10},{10,8},{12,14},{14,12},{1,3},{3,1},... | collective-permute-start | bytes 786440 | tf_op jit(solution)/shard_map/ppermute | solution.py:54
  313.6 23.0 %collective-permute-start.6 = (bf16[64,2048]{1,0:T(8,128)(2,1)S(1)}, bf16[64,2048]{1,0:T(8,128)(2,1)S(1)}, u32[]{:S(2)}, u32[]{:S(2)}) collective-permute-start(bf16[64,2048]{1,0:T(8,128)(2,1)S(1)} %pad_maximum_fusion.12), channel_id=1, source_target_pairs={{0,18},{2,16},{4,22},{6,20},{8,26},{10,24},{12,30},{14,28},{16,2},... | collective-permute-start | bytes 786440 | tf_op jit(solution)/shard_map/ppermute | solution.py:60
  333.1 23.4 %collective-permute-start.17 = (bf16[64,2048]{1,0:T(8,128)(2,1)}, bf16[64,2048]{1,0:T(8,128)(2,1)S(1)}, u32[]{:S(2)}, u32[]{:S(2)}) collective-permute-start(bf16[64,2048]{1,0:T(8,128)(2,1)} %get-tuple-element.89), channel_id=1, source_target_pairs={{0,2},{2,0},{4,6},{6,4},{8,10},{10,8},{12,14},{14,12},{1,3},{3,1},... | collective-permute-start | bytes 786440 | tf_op jit(solution)/shard_map/ppermute | solution.py:54
  334.6 23.7 %collective-permute-start.18 = (bf16[64,2048]{1,0:T(8,128)(2,1)}, bf16[64,2048]{1,0:T(8,128)(2,1)S(1)}, u32[]{:S(2)}, u32[]{:S(2)}) collective-permute-start(bf16[64,2048]{1,0:T(8,128)(2,1)} %get-tuple-element.90), channel_id=1, source_target_pairs={{0,16},{16,0},{1,17},{17,1},{2,18},{18,2},{3,19},{19,3},{4,20},{20... | collective-permute-start | bytes 786440 | tf_op jit(solution)/shard_map/ppermute | solution.py:50
  343.7 30.6 %collective-permute-start.10 = (bf16[64,2048]{1,0:T(8,128)(2,1)}, bf16[64,2048]{1,0:T(8,128)(2,1)S(1)}, u32[]{:S(2)}, u32[]{:S(2)}) collective-permute-start(bf16[64,2048]{1,0:T(8,128)(2,1)} %get-tuple-element.87), channel_id=1, source_target_pairs={{0,18},{2,16},{4,22},{6,20},{8,26},{10,24},{12,30},{14,28},{16,2},... | collective-permute-start | bytes 786440 | tf_op jit(solution)/shard_map/ppermute | solution.py:60
  346.5 27.7 %collective-permute-start.8 = (bf16[64,2048]{1,0:T(8,128)(2,1)}, bf16[64,2048]{1,0:T(8,128)(2,1)S(1)}, u32[]{:S(2)}, u32[]{:S(2)}) collective-permute-start(bf16[64,2048]{1,0:T(8,128)(2,1)} %get-tuple-element.85), channel_id=1, source_target_pairs={{0,2},{2,0},{4,6},{6,4},{8,10},{10,8},{12,14},{14,12},{1,3},{3,1},... | collective-permute-start | bytes 786440 | tf_op jit(solution)/shard_map/ppermute | solution.py:54
  358.5 23.5 %collective-permute-start.20 = (bf16[32,2048]{1,0:T(8,128)(2,1)S(1)}, bf16[32,2048]{1,0:T(8,128)(2,1)S(1)}, u32[]{:S(2)}, u32[]{:S(2)}) collective-permute-start(bf16[32,2048]{1,0:T(8,128)(2,1)S(1)} %get-tuple-element.249), channel_id=1, source_target_pairs={{0,8},{2,10},{4,12},{6,14},{8,0},{10,2},{12,4},{14,6},{1,9},{3,11}... | collective-permute-start | bytes 393224 | tf_op jit(solution)/shard_map/ppermute | solution.py:54
  418.9 177.9 %all-gather.13.cloned.1.call-start = ((), (), s32[]{:S(2)}) async-start(), calls=%async_computation.7 | async-start | bytes 1769472 | tf_op jit(solution)/shard_map/all_gather | solution.py:790
  534.0 58.4 %collective-permute-start.55 = (bf16[8,3,256,256]{3,2,1,0:T(8,128)(2,1)}, bf16[8,3,256,256]{3,2,1,0:T(8,128)(2,1)}, u32[]{:S(2)}, u32[]{:S(2)}) collective-permute-start(bf16[8,3,256,256]{3,2,1,0:T(8,128)(2,1)} %get-tuple-element.121), channel_id=1, source_target_pairs={{0,1},{1,0},{2,3},{3,2},{4,5},{5,4},{6,7},{7,6},{8,9},{9,8},{10,11... | collective-permute-start | bytes 9437192 | tf_op jit(solution)/shard_map/ppermute | solution.py:46
  534.0 191.6 %reduce-scatter.2.cloned.1.call-start = ((), (), s32[]{:S(2)}) async-start(), calls=%async_computation.6 | async-start | bytes 1179648 | tf_op jit(solution)/shard_map/reduce_scatter | solution.py:827
  549.2 94.0 %collective-permute-start.48 = (bf16[256,2048]{1,0:T(8,128)(2,1)}, bf16[256,2048]{1,0:T(8,128)(2,1)}, u32[]{:S(2)}, u32[]{:S(2)}) collective-permute-start(bf16[256,2048]{1,0:T(8,128)(2,1)} %slice.236), channel_id=1, source_target_pairs={{0,16},{16,0},{1,17},{17,1},{2,18},{18,2},{3,19},{19,3},{4,20},{20... | collective-permute-start | bytes 3145736 | tf_op jit(solution)/shard_map/ppermute | solution.py:50
  556.3 24.9 %collective-permute-start.53 = (bf16[64,2048]{1,0:T(8,128)(2,1)S(1)}, bf16[64,2048]{1,0:T(8,128)(2,1)S(1)}, u32[]{:S(2)}, u32[]{:S(2)}) collective-permute-start(bf16[64,2048]{1,0:T(8,128)(2,1)S(1)} %get-tuple-element.252), channel_id=1, source_target_pairs={{0,16},{16,0},{1,17},{17,1},{2,18},{18,2},{3,19},{19,3},{4,20},{20... | collective-permute-start | bytes 786440 | tf_op jit(solution)/shard_map/ppermute | solution.py:50
  557.2 30.6 %collective-permute-start.54 = (bf16[64,2048]{1,0:T(8,128)(2,1)S(1)}, bf16[64,2048]{1,0:T(8,128)(2,1)S(1)}, u32[]{:S(2)}, u32[]{:S(2)}) collective-permute-start(bf16[64,2048]{1,0:T(8,128)(2,1)S(1)} %get-tuple-element.252), channel_id=1, source_target_pairs={{0,18},{2,16},{4,22},{6,20},{8,26},{10,24},{12,30},{14,28},{16,2},... | collective-permute-start | bytes 786440 | tf_op jit(solution)/shard_map/ppermute | solution.py:60
  560.1 28.2 %collective-permute-start.62 = (bf16[64,2048]{1,0:T(8,128)(2,1)}, bf16[64,2048]{1,0:T(8,128)(2,1)S(1)}, u32[]{:S(2)}, u32[]{:S(2)}) collective-permute-start(bf16[64,2048]{1,0:T(8,128)(2,1)} %get-tuple-element.255), channel_id=1, source_target_pairs={{0,2},{2,0},{4,6},{6,4},{8,10},{10,8},{12,14},{14,12},{1,3},{3,1},... | collective-permute-start | bytes 786440 | tf_op jit(solution)/shard_map/ppermute | solution.py:54
  651.0 24.7 %all-to-all-start.1 = ((bf16[1,128,8,256]{3,1,0,2:T(8,128)(2,1)}), bf16[1,128,8,256]{3,1,0,2:T(8,128)(2,1)S(1)}, u32[]{:S(2)}, u32[]{:S(2)}) async-start(bf16[1,128,8,256]{3,1,0,2:T(8,128)(2,1)} %copy.49), calls=%async_computation.2 | async-start | bytes 1048576 | tf_op jit(solution)/shard_map/all_to_all | solution.py:843
  676.5 172.1 %all-to-all-start.2 = ((bf16[16,3,256,256]{3,2,1,0:T(8,128)(2,1)}), bf16[16,3,256,256]{3,2,1,0:T(8,128)(2,1)}, u32[]{:S(2)}, u32[]{:S(2)}) async-start(bf16[16,3,256,256]{3,2,1,0:T(8,128)(2,1)} %shard_map.212), calls=%async_computation.3 | async-start | bytes 12582912 | tf_op jit(solution)/shard_map/all_to_all | solution.py:882
  681.1 145.3 %all-gather.15.cloned.1.call-start = ((), (), s32[]{:S(2)}) async-start(), calls=%async_computation.8 | async-start | bytes 1769472 | tf_op jit(solution)/shard_map/all_gather | solution.py:790
  741.2 37.6 %collective-permute-start.77 = (bf16[64,2048]{1,0:T(8,128)(2,1)}, bf16[64,2048]{1,0:T(8,128)(2,1)}, u32[]{:S(2)}, u32[]{:S(2)}) collective-permute-start(bf16[64,2048]{1,0:T(8,128)(2,1)} %get-tuple-element.251), channel_id=1, source_target_pairs={{0,1},{1,0},{2,3},{3,2},{4,5},{5,4},{6,7},{7,6},{8,9},{9,8},{10,11... | collective-permute-start | bytes 786440 | tf_op jit(solution)/shard_map/ppermute | solution.py:46
  (123 other events, 1536.5 us)
Sparse Core Ops, SparseCore 0:
  11.4 111.4 all-gather.8
  125.6 134.5 all-gather.16
  262.9 138.4 all-gather.18
  419.0 80.2 all-gather.10
  534.1 52.2 all-gather.12
  646.0 79.5 reduce-scatter.1
  761.4 65.0 all-gather.14
